TPU v7x, 32 devices: a whole 2x2x4 slice. The times are simulated.
32 devices in a mesh: dom: 8 (over z, x), hid: 4 (over y, core).
Axes of the slice: x: 2, y: 2, z: 4, core: 2. Of those that a mesh axis runs over, the one named last changes fastest.
Arguments:
- particles: bfloat16 [8, 1026, 4096], P('dom', None, 'hid')
- noise: bfloat16 [8, 1026, 4096], P('dom', None, 'hid'), may hold values from -5 to 5
- ancestors: int32 [8], P('dom'), may hold values from 0 to 7
- accepted: int32 [8], P('dom'), may hold values 0 or 1
- data: bfloat16 [320, 1024], replicated, may hold values from -6 to 6
- targets: float32 [320], replicated, may hold values from -6 to 6
Outputs:
- moved: bfloat16 [8, 1026, 4096], P('dom', None, 'hid')
- fit: float32 [8], P('dom')
All inputs are finite; a program needn't handle non-finite values. No bound on the sum of `accepted` on one device may be relied on, other than what follows from the above.
Results may differ from a plain program's by a relative error of at most 0.0036.
Values may be sent and summed in bfloat16 or wider, within the bound.
A program may use at most 128 MiB of HBM per device.

v0:
```python
import jax
import jax.numpy as jnp
from jax import lax
from jax.sharding import PartitionSpec as P

LEAPFROG = 2


TEMPER_LEVEL = 0.125
NOISE_INV_VARIANCE = 4.0
STEP_SIZE = 0.4


def body(particles, noise, ancestors, accepted, data, targets):
    groups = lax.axis_size("dom")
    per_device = particles.shape[0]
    rows_all = particles.shape[1]
    hid_width = particles.shape[2]
    particle_total = groups * per_device
    flattened = particles.reshape(per_device, rows_all * hid_width)
    lineage = lax.all_gather(ancestors, "dom", axis=0, tiled=True)
    spread = lax.all_to_all(flattened, "dom", split_axis=1, concat_axis=0, tiled=True)
    chosen = jnp.take(spread, lineage, axis=0)
    returned = lax.all_to_all(chosen, "dom", split_axis=0, concat_axis=1, tiled=True)
    resampled = returned.reshape(per_device, rows_all, hid_width)
    shrink = particle_total / (particle_total + 5.0)
    floor_term = 0.001 * 5.0 / (particle_total + 5.0)
    widened = chosen.astype(jnp.float32)
    mean_value = jnp.sum(widened, axis=0) / particle_total
    mean_square = jnp.sum(widened * widened, axis=0) / particle_total
    mass_share = (shrink * (mean_square - mean_value * mean_value) + floor_term).astype(
        jnp.bfloat16
    )
    inv_mass = (
        lax.all_gather(mass_share, "dom", axis=0, tiled=True)
        .reshape(rows_all, hid_width)
        .astype(jnp.float32)
    )
    in_scale = data.shape[1] ** (-0.5)
    out_scale = (hid_width * lax.axis_size("hid")) ** (-0.5)

    def compute_potential(position):
        weights = position[:, :-2, :].astype(jnp.bfloat16)
        preact = (
            jnp.einsum("rd,pdh->prh", data, weights, preferred_element_type=jnp.float32) * in_scale
            + position[:, -2:-1, :]
        )
        hidden = jnp.tanh(preact)
        partial_value = (
            jnp.einsum("prh,ph->pr", hidden, position[:, -1, :], precision=lax.Precision.HIGHEST)
            * out_scale
        )
        network_outputs = lax.psum(partial_value, "hid")
        return (hidden, network_outputs)

    def potential_gradient(position, hidden, network_outputs):
        fit_residual = TEMPER_LEVEL * NOISE_INV_VARIANCE * (network_outputs - targets[None, :])
        out_weight = position[:, -1, :]
        grad_out = (
            jnp.einsum("pr,prh->ph", fit_residual, hidden, precision=lax.Precision.HIGHEST)
            * out_scale
            + out_weight
        )
        backward = (
            fit_residual[:, :, None]
            * (out_weight * out_scale)[:, None, :]
            * (1.0 - hidden * hidden)
        )
        grad_bias = jnp.sum(backward, axis=1) + position[:, -2, :]
        grad_weight = (
            jnp.einsum(
                "rd,prh->pdh",
                data,
                backward.astype(jnp.bfloat16),
                preferred_element_type=jnp.float32,
            )
            * in_scale
            + position[:, :-2, :]
        )
        return jnp.concatenate([grad_weight, grad_bias[:, None, :], grad_out[:, None, :]], axis=1)

    position0 = resampled.astype(jnp.float32)
    momentum = noise.astype(jnp.float32) / jnp.sqrt(inv_mass)[None]
    hidden, initial_outputs0 = compute_potential(position0)
    grad = potential_gradient(position0, hidden, initial_outputs0)
    position = position0
    network_outputs = initial_outputs0
    for section in range(LEAPFROG):
        momentum = momentum - 0.5 * STEP_SIZE * grad
        position = position + STEP_SIZE * inv_mass[None] * momentum
        hidden, network_outputs = compute_potential(position)
        if section + 1 < LEAPFROG:
            grad = potential_gradient(position, hidden, network_outputs)
            momentum = momentum - 0.5 * STEP_SIZE * grad
    fit_start = jnp.mean(jnp.square(targets[None, :] - initial_outputs0), axis=1)
    fit_end = jnp.mean(jnp.square(targets[None, :] - network_outputs), axis=1)
    keep = accepted == 1
    moved = jnp.where(keep[:, None, None], position, position0).astype(jnp.bfloat16)
    fit = jnp.where(keep, fit_end, fit_start)
    return (moved, fit)


def solution(mesh):
    return jax.shard_map(
        body,
        mesh=mesh,
        in_specs=(P("dom", None, "hid"), P("dom", None, "hid"), P("dom"), P("dom"), P(), P()),
        out_specs=(P("dom", None, "hid"), P("dom")),
        check_vma=False,
    )
```

profile of v0, /device:TPU:0, one launch (start us, length us, event | category | flops | bytes accessed | tf_op | source)
XLA Modules:
  0.0 346.9 jit_solution(13278493467613272018)
XLA Ops:
  7.2 5.4 %all_to_all.24 = bf16[1,8,131328]{2,0,1:T(2,128)(2,1)} reshape(bf16[1,1026,1024]{2,1,0:T(8,128)(2,1)} %param.6) | data formatting | bytes 4202496 | tf_op jit(solution)/shard_map/all_to_all | solution.py:22
  13.1 13.5 %reduce.19 = bf16[8,131328]{1,0:T(8,128)(2,1)S(1)} reduce(bf16[8,1,131328]{2,1,0:T(2,128)(2,1)} %bitcast.163, bf16[]{:T(256)} %broadcast.282), dimensions={1}, to_apply=%bitcast.154.reduce_sub_computation | reduce | bytes 4202498
  26.6 1.9 reshape.462
  28.5 7.4 %all-to-all-start = ((bf16[8,2,65664]{2,1,0:T(2,128)(2,1)}), bf16[8,2,65664]{2,1,0:T(2,128)(2,1)S(1)}, u32[]{:S(2)}, u32[]{:S(2)}) async-start(bf16[8,2,65664]{2,1,0:T(2,128)(2,1)} %reshape.462), calls=%async_computation | async-start | bytes 4202496 | tf_op jit(solution)/shard_map/all_to_all | solution.py:22
  37.2 0.8 dynamic-update-slice
  38.0 46.9 %all-reduce = s32[8]{0:T(128)S(1)} all-reduce(s32[8]{0:T(128)S(1)} %dynamic-update-slice), channel_id=1, replica_groups=mesh['dom'=8,'hid'=4] {'dom'}, use_global_device_ids=true, to_apply=%add | all-reduce | flops 8 | bytes 64
  84.9 7.2 %reshape.463 = bf16[8,1,131328]{2,1,0:T(2,128)(2,1)} reshape(bf16[8,2,65664]{2,1,0:T(2,128)(2,1)S(1)} %all-to-all-done) | data formatting | bytes 4202496
  92.1 2.8 copy.15
  95.1 2.3 gather_fusion
  97.3 2.3 constant_dynamic-update-slice_fusion.1
  99.6 1.3 gather_fusion.1
  100.9 1.0 constant_dynamic-update-slice_fusion
  102.0 1.9 bitcast_select_fusion
  104.2 7.5 %fusion.2 = (f32[131328]{0:T(1024)S(1)}, f32[131328]{0:T(1024)}) fusion(bf16[8,131328]{1,0:T(8,128)(2,1)S(1)} %copy-done.7, pred[8]{0:T(512)(128)(4,1)S(1)} %compare_and_fusion), kind=kLoop, calls=%fused_computation.10 | loop fusion | flops 4990464 | bytes 3151880 | tf_op jit(solution)/shard_map/reduce_sum | solution.py:30
  111.6 2.9 reduce.20
  114.6 3.5 %reshape.464 = bf16[8,2,65664]{2,1,0:T(2,128)(2,1)} reshape(bf16[8,131328]{1,0:T(8,128)(2,1)} %reduce.20) | data formatting | bytes 4202496
  118.1 3.6 %all-to-all-start.1 = ((bf16[8,2,65664]{2,1,0:T(2,128)(2,1)}), bf16[8,2,65664]{2,1,0:T(2,128)(2,1)S(1)}, u32[]{:S(2)}, u32[]{:S(2)}) async-start(bf16[8,2,65664]{2,1,0:T(2,128)(2,1)} %reshape.464), calls=%async_computation.1 | async-start | bytes 4202496 | tf_op jit(solution)/shard_map/all_to_all | solution.py:24
  122.0 1.2 add_convert_fusion
  123.2 3.7 %reshape.431 = bf16[1,1,131328]{2,1,0:T(2,128)(2,1)} reshape(bf16[131328]{0:T(1024)(128)(2,1)S(1)} %add_convert_fusion) | data formatting | bytes 525312
  127.6 59.6 %all-to-all-done.1 = bf16[8,2,65664]{2,1,0:T(2,128)(2,1)S(1)} async-done(((bf16[8,2,65664]{2,1,0:T(2,128)(2,1)}), bf16[8,2,65664]{2,1,0:T(2,128)(2,1)S(1)}, u32[]{:S(2)}, u32[]{:S(2)}) %all-to-all-start.1) | async-done | bytes 2101280 | tf_op jit(solution)/shard_map/all_to_all | solution.py:24
  187.1 7.2 %reshape.465 = bf16[8,1,131328]{2,1,0:T(2,128)(2,1)} reshape(bf16[8,2,65664]{2,1,0:T(2,128)(2,1)S(1)} %all-to-all-done.1) | data formatting | bytes 4202496
  194.3 14.1 %reduce.4 = bf16[8,131328]{1,0:T(8,128)(2,1)} reduce(bf16[8,1,131328]{2,1,0:T(2,128)(2,1)} %reshape.465, bf16[]{:T(256)} %constant.58), dimensions={1}, to_apply=%all_to_all.23.reduce_sub_computation | reduce | bytes 4202498 | tf_op jit(solution)/shard_map/all_to_all | solution.py:24
  208.4 4.7 %reshape.398 = bf16[1,1026,1024]{2,1,0:T(8,128)(2,1)S(1)} reshape(bf16[8,131328]{1,0:T(8,128)(2,1)} %reduce.4) | data formatting | bytes 4202496 | tf_op jit(solution)/shard_map/reshape | solution.py:25
  213.7 0.9 fusion.33
  214.6 1.0 copy-done.2
  216.6 6.2 %psum.21 = f32[1,320]{1,0:T(1,128)S(1)} all-reduce(f32[1,320]{1,0:T(1,128)S(1)} %mul.210), channel_id=1, replica_groups=mesh['dom'=8,'hid'=4] {'hid'}, use_global_device_ids=true, to_apply=%region_2.3 | all-reduce | flops 320 | bytes 2560 | tf_op jit(solution)/shard_map/psum | solution.py:53
  223.5 0.8 broadcast_multiply_fusion.1
  224.3 1.6 fusion.69
  225.8 0.8 slice_add_fusion.1
  226.6 2.0 fusion.57
  228.6 5.5 %bitcast_add_fusion.1 = f32[1,1024,1024]{2,1,0:T(8,128)} fusion(f32[1,1026,1024]{2,1,0:T(8,128)} %copy-done.2, bf16[320,1024]{1,0:T(8,128)(2,1)S(1)} %copy-done, f32[1,1024,320]{1,2,0:T(8,128)S(1)} %copy-done.4, f32[1024]{0:T(1024)S(1)} %bitcast.169, f32[320]{0:T(512)S(1)} %get-tuple-element.7), kind=kOutput, calls=%fused_computation.15 | convolution fusion | flops 674824192 | bytes 10360064 | tf_op jit(solution)/shard_map/rd,prh->pdh/dot_general | solution.py:71
  234.2 27.5 %rsqrt_reduce_fusion = (f32[8,131328]{1,0:T(8,128)}, f32[8,131328]{1,0:T(8,128)}) fusion(bf16[8,1,131328]{2,1,0:T(2,128)(2,1)} %all-gather.3.cloned.1.call-done), kind=kLoop, calls=%fused_computation.11 | loop fusion | flops 2101248 | bytes 10506240 | tf_op jit(solution)/shard_map/sqrt | solution.py:83
  261.7 5.3 %mul.206 = f32[1,1026,1024]{2,1,0:T(8,128)} reshape(f32[8,131328]{1,0:T(8,128)} %get-tuple-element.3) | data formatting | bytes 8404992 | tf_op jit(solution)/shard_map/mul | solution.py:90
  267.0 5.3 %sqrt.7 = f32[1,1026,1024]{2,1,0:T(8,128)} reshape(f32[8,131328]{1,0:T(8,128)} %get-tuple-element.2) | data formatting | bytes 8404992 | tf_op jit(solution)/shard_map/sqrt | solution.py:83
  272.3 11.0 %concatenate.27 = f32[1,1026,1024]{2,1,0:T(8,128)} concatenate(f32[1,1024,1024]{2,1,0:T(8,128)} %bitcast_add_fusion.1, f32[1,1,1024]{2,1,0:T(1,128)S(1)} %slice_add_fusion.1, f32[1,1,1024]{2,1,0:T(1,128)S(1)} %bitcast.170), dimensions={1} | concatenate | bytes 8404992 | tf_op jit(solution)/shard_map/concatenate | solution.py:80
  283.3 7.2 %multiply_add_fusion = f32[1,1026,1024]{2,1,0:T(8,128)S(1)} fusion(f32[1,1026,1024]{2,1,0:T(8,128)} %mul.206, bf16[1,1026,1024]{2,1,0:T(8,128)(2,1)S(1)} %reshape.398, f32[1,1026,1024]{2,1,0:T(8,128)} %concatenate.27, f32[1,1026,1024]{2,1,0:T(8,128)} %sqrt.7, bf16[1,1026,1024]{2,1,0:T(8,128)(2,1)} %param.7), kind=kLoop, calls=%fused_computation.8 | loop fusion | flops 7354368 | bytes 21012480 | tf_op jit(solution)/shard_map/add | solution.py:90
  290.5 0.9 fusion.39
  291.4 1.1 copy-done.1
  292.4 1.1 fusion.66
  293.6 6.2 %psum.22 = f32[1,320]{1,0:T(1,128)S(1)} all-reduce(f32[1,320]{1,0:T(1,128)S(1)} %mul.229), channel_id=1, replica_groups=mesh['dom'=8,'hid'=4] {'hid'}, use_global_device_ids=true, to_apply=%region_4.5 | all-reduce | flops 320 | bytes 2560 | tf_op jit(solution)/shard_map/psum | solution.py:53
  299.8 2.1 fusion.51
  302.3 5.5 %bitcast_add_fusion = f32[1,1024,1024]{2,1,0:T(8,128)} fusion(f32[1,1026,1024]{2,1,0:T(8,128)} %copy-done.1, bf16[320,1024]{1,0:T(8,128)(2,1)S(1)} %copy-done, f32[1,1024,320]{1,2,0:T(8,128)S(1)} %copy-done.6, f32[1024]{0:T(1024)S(1)} %bitcast.167, f32[320]{0:T(512)S(1)} %fusion.89), kind=kOutput, calls=%fused_computation.14 | convolution fusion | flops 674824192 | bytes 10360064 | tf_op jit(solution)/shard_map/rd,prh->pdh/dot_general | solution.py:71
  307.8 0.8 slice_add_fusion
  308.6 10.7 %concatenate.29 = f32[1,1026,1024]{2,1,0:T(8,128)} concatenate(f32[1,1024,1024]{2,1,0:T(8,128)} %bitcast_add_fusion, f32[1,1,1024]{2,1,0:T(1,128)S(1)} %slice_add_fusion, f32[1,1,1024]{2,1,0:T(1,128)S(1)} %bitcast.171), dimensions={1} | concatenate | bytes 8404992 | tf_op jit(solution)/shard_map/concatenate | solution.py:80
  319.3 9.1 %select_convert_fusion = (bf16[1,1026,1024]{2,1,0:T(8,128)(2,1)}, f32[1,1026,1024]{2,1,0:T(8,128)S(1)}) fusion(bf16[1,1026,1024]{2,1,0:T(8,128)(2,1)S(1)} %reshape.398, pred[]{:T(512)} %bitcast, f32[1,1026,1024]{2,1,0:T(8,128)} %mul.206, f32[1,1026,1024]{2,1,0:T(8,128)} %concatenate.29, f32[1,1026,1024]{2,1,0:T(8,128)} %concatenate.27, ...), kind=kLoop, calls=%fused_computation.7 | loop fusion | flops 13658112 | bytes 27316224 | tf_op jit(solution)/shard_map/convert_element_type | solution.py:98
  328.4 0.9 fusion.48
  329.3 1.2 convolution_reduce_fusion
  330.5 6.1 %psum.23 = f32[1,320]{1,0:T(1,128)S(1)} all-reduce(f32[1,320]{1,0:T(1,128)S(1)} %mul.248), channel_id=1, replica_groups=mesh['dom'=8,'hid'=4] {'hid'}, use_global_device_ids=true, to_apply=%region_6.7 | all-reduce | flops 320 | bytes 2560 | tf_op jit(solution)/shard_map/psum | solution.py:53
  (46 shorter events, 5.1 us)
Async XLA Ops:
  7.2 206.5 %copy-start = (bf16[320,1024]{1,0:T(8,128)(2,1)S(1)}, bf16[320,1024]{1,0:T(8,128)(2,1)}, u32[]{:S(2)}) copy-start(bf16[320,1024]{1,0:T(8,128)(2,1)} %param.10) | copy-start | bytes 1966084
  28.5 8.0 %copy-start.9 = (u32[32]{0:T(128)S(1)}, u32[32]{0:T(128)}, u32[]{:S(2)}) copy-start(u32[32]{0:T(128)} %constant.54) | copy-start | bytes 388
  28.5 56.4 %all-to-all-start = ((bf16[8,2,65664]{2,1,0:T(2,128)(2,1)}), bf16[8,2,65664]{2,1,0:T(2,128)(2,1)S(1)}, u32[]{:S(2)}, u32[]{:S(2)}) async-start(bf16[8,2,65664]{2,1,0:T(2,128)(2,1)} %reshape.462), calls=%async_computation | async-start | bytes 4202496 | tf_op jit(solution)/shard_map/all_to_all | solution.py:22
  102.0 2.2 copy-start.7
  118.1 69.0 %all-to-all-start.1 = ((bf16[8,2,65664]{2,1,0:T(2,128)(2,1)}), bf16[8,2,65664]{2,1,0:T(2,128)(2,1)S(1)}, u32[]{:S(2)}, u32[]{:S(2)}) async-start(bf16[8,2,65664]{2,1,0:T(2,128)(2,1)} %reshape.464), calls=%async_computation.1 | async-start | bytes 4202496 | tf_op jit(solution)/shard_map/all_to_all | solution.py:24
  121.8 112.4 %all-gather.3.cloned.1.call-start = ((), (), s32[]{:S(2)}) async-start(), calls=%async_computation.2 | async-start | bytes 4727808 | tf_op jit(solution)/shard_map/all_gather | solution.py:35
  213.6 1.9 copy-start.2
  213.7 9.2 %copy-start.8 = (f32[320]{0:T(512)S(1)}, f32[320]{0:T(512)}, u32[]{:S(2)}) copy-start(f32[320]{0:T(512)} %param.11) | copy-start | bytes 3844
  215.6 1.1 copy-start.3
  222.9 5.8 %copy-start.4 = (f32[1,1024,320]{1,2,0:T(8,128)S(1)}, f32[1,1024,320]{1,2,0:T(8,128)}, u32[]{:S(2)}) copy-start(f32[1,1024,320]{1,2,0:T(8,128)} %copy-done.3) | copy-start | bytes 3932164
  290.5 1.9 copy-start.1
  292.4 1.2 copy-start.5
  299.8 2.2 copy-start.6
Sparse Core Ops, SparseCore 0:
  127.0 98.5 all-gather.2
where the time goes:
time: 352 us; the launch traced here: 347 us
  other arithmetic  90.7 us (26%)
  local copies, waits for them, and re-layouts  80.6 us (23%)
  blocking collectives  65.4 us (19%)
  waiting for transfers between devices  59.6 us (17%)
  matrix products  20.9 us (6%)
  between operations  18.3 us (5%)
  starting transfers between devices  11.2 us (3%)
    all_to_all x1, waiting for transfers between devices, body(): lax.all_to_all(chosen, 'dom', split_axis=0, concat_axis=1, tiled=True)  59.6 us
    unnamed x1, blocking collectives  46.9 us
    unnamed x32, local copies, waits for them, and re-layouts  34.3 us
    sqrt x1, other arithmetic, body(): momentum = noise.astype(jnp.float32) / jnp.sqrt(inv_mass)[None]  27.5 us
    concatenate x2, local copies, waits for them, and re-layouts, potential_gradient(): jnp.concatenate([grad_weight, grad_bias[:, None, :], grad_out[:, None, :]...  21.7 us
    psum x3, blocking collectives, compute_potential(): network_outputs = lax.psum(partial_value, 'hid')  18.6 us
    all_to_all x1, other arithmetic, body(): lax.all_to_all(chosen, 'dom', split_axis=0, concat_axis=1, tiled=True)  14.1 us
    unnamed x1, other arithmetic  13.5 us
  transfers between devices with their start and end apart: 3, of which 1 were waited for; matrix products, arithmetic and copies ran while one was open for 13% of the time, Pallas kernels for 0%

commit v1 on v0

v1 whole, which is shorter than its diff:
```python
import functools

import jax
import jax.numpy as jnp
from jax import lax
from jax.experimental import pallas as pl
from jax.experimental.pallas import tpu as pltpu
from jax.sharding import PartitionSpec as P

TEMPER_LEVEL = 0.125
NOISE_INV_VARIANCE = 4.0
STEP_SIZE = 0.4
MESH = pl.DeviceIdType.MESH
TILE = 256
CHUNK = 16


def kernel(
    groups, hids,
    anc_ref, acc_ref, tail_ref, part_ref, noise_ref, data_ref, tgt_ref,
    main_out, tail_out, fit_out,
    anc_all, anc_s, tails, recv, picked, theta0, mass, noise_v, mom, pos, moved, hid, resid,
    tpos, tpos0, tmom, tinv, tout, part_buf, part_all,
    anc_ss, anc_rs, tail_ss, tail_rs, p_ss, p_rs, q_ss, q_rs,
    up_ss, down_ss, side_ss, mass_rs, h_ss, h_rs, loc,
):
    me = lax.axis_index("dom")
    my_hid = lax.axis_index("hid")
    depth, width = theta0.shape
    rows = depth // groups
    data_rows = data_ref.shape[0]
    padded = part_buf.shape[-1]
    in_scale = depth ** (-0.5)
    out_scale = (width * hids) ** (-0.5)
    half = groups // 2
    offsets = []
    for s in range(groups - 1):
        offsets.append(half + (s + 1) // 2 * (1 if s % 2 else -1))

    def wrap(i, n):
        return lax.rem(i, n)

    def block(i):
        return pl.ds(pl.multiple_of(i * rows, rows), rows)

    noise_copy = pltpu.make_async_copy(noise_ref.at[0, pl.ds(0, depth)], noise_v, loc.at[0])
    noise_copy.start()
    own_copy = pltpu.make_async_copy(part_ref.at[0, block(me)], recv.at[me], loc.at[1])
    own_copy.start()
    anc_all[me] = anc_ref[...]
    tails[me] = tail_ref[...]

    barrier = pltpu.get_barrier_semaphore()
    for k in range(1, groups):
        pl.semaphore_signal(barrier, inc=1, device_id=(wrap(me + k, groups), my_hid), device_id_type=MESH)
    for k in range(1, hids):
        pl.semaphore_signal(barrier, inc=1, device_id=(me, wrap(my_hid + k, hids)), device_id_type=MESH)
    pl.semaphore_wait(barrier, groups - 1 + hids - 1)

    def anc_copy(t, slot):
        return pltpu.make_async_remote_copy(
            anc_all.at[slot], anc_all.at[slot], anc_ss.at[t], anc_rs.at[slot],
            device_id=(t, my_hid), device_id_type=MESH)

    def tail_copy(t, slot):
        return pltpu.make_async_remote_copy(
            tails.at[slot], tails.at[slot], tail_ss.at[t], tail_rs.at[slot],
            device_id=(t, my_hid), device_id_type=MESH)

    def part_copy(t, slot):
        return pltpu.make_async_remote_copy(
            part_ref.at[0, block(t)], recv.at[slot], p_ss.at[t], p_rs.at[slot],
            device_id=(t, my_hid), device_id_type=MESH)

    def pick_copy(t, slot):
        return pltpu.make_async_remote_copy(
            picked.at[t], theta0.at[block(slot)], q_ss.at[t], q_rs.at[slot],
            device_id=(t, my_hid), device_id_type=MESH)

    for k in offsets:
        t = wrap(me + k, groups)
        anc_copy(t, me).start()
    for k in offsets:
        t = wrap(me + k, groups)
        part_copy(t, me).start()
    for k in offsets:
        t = wrap(me + k, groups)
        tail_copy(t, me).start()

    for k in offsets:
        s = wrap(me + groups - k, groups)
        anc_copy(s, s).wait_recv()
    scalars = pltpu.make_async_copy(anc_all, anc_s, loc.at[2])
    scalars.start()
    scalars.wait()
    own_copy.wait()
    for k in offsets:
        s = wrap(me + groups - k, groups)
        part_copy(s, s).wait_recv()

    shrink = groups / (groups + 5.0)
    floor_term = 0.001 * 5.0 / (groups + 5.0)

    def finish(total, square):
        mean = total / groups
        return (shrink * (square / groups - mean * mean) + floor_term).astype(jnp.bfloat16)

    my_rows = block(me)

    @pl.loop(0, rows // CHUNK)
    def _(r):
        here = pl.ds(pl.multiple_of(r * CHUNK, CHUNK), CHUNK)

        def add(i, carry):
            total, square = carry
            got = recv[anc_s[i, 0, 0], here]
            picked[i, here] = got
            wide = got.astype(jnp.float32)
            return total + wide, square + wide * wide

        zero = jnp.zeros((CHUNK, width), jnp.float32)
        carry = (zero, zero)
        if groups <= 8:
            for i in range(groups):
                carry = add(i, carry)
        else:
            carry = lax.fori_loop(0, groups, add, carry)
        mass[pl.ds(pl.multiple_of(me * rows + r * CHUNK, CHUNK), CHUNK)] = finish(*carry)
        theta0[pl.ds(pl.multiple_of(me * rows + r * CHUNK, CHUNK), CHUNK)] = picked[me, here]

    place, inner = me // 2, lax.rem(me, 2)

    def mass_copy(t, who, sem):
        return pltpu.make_async_remote_copy(
            mass.at[block(who)], mass.at[block(who)], sem.at[who], mass_rs.at[who],
            device_id=(t, my_hid), device_id_type=MESH)

    def spread(who, up, down):
        if up:
            @pl.when(place < half - 1)
            def _():
                mass_copy(me + 2, who, up_ss).start()
        if down:
            @pl.when(place > 0)
            def _():
                mass_copy(me - 2, who, down_ss).start()
        mass_copy(me + 1 - 2 * inner, who, side_ss).start()

    spread(me, True, True)
    for k in offsets:
        pick_copy(wrap(me + k, groups), me).start()

    for k in offsets:
        s = wrap(me + groups - k, groups)
        tail_copy(s, s).wait_recv()

    def add_tail(i, carry):
        total, square = carry
        wide = tails[anc_s[i, 0, 0]].astype(jnp.float32)
        return total + wide, square + wide * wide

    zero = jnp.zeros((16, width), jnp.float32)
    tinv[...] = finish(*lax.fori_loop(0, groups, add_tail, (zero, zero))).astype(jnp.float32)
    tpos0[...] = tails[anc_s[me, 0, 0]].astype(jnp.float32)
    tpos[...] = tpos0[...]
    tmom[0:2] = tail_ref[...].astype(jnp.float32)[2:4] * lax.rsqrt(tinv[0:2])

    for s in range(1, half):
        @pl.when(place >= s)
        def _():
            mass_copy(me, me - 2 * s, up_ss).wait_recv()
            spread(me - 2 * s, True, False)

        @pl.when(place + s < half)
        def _():
            mass_copy(me, me + 2 * s, up_ss).wait_recv()
            spread(me + 2 * s, False, True)

    for k in offsets:
        s = wrap(me + groups - k, groups)
        pick_copy(s, s).wait_recv()

    data = data_ref[...]

    def forward(weights, cols, keep_hidden):
        pre = jnp.dot(data_ref[...], weights, preferred_element_type=jnp.float32)
        h = jnp.tanh(pre * in_scale + tpos[0:1, cols])
        if keep_hidden:
            hid[:, cols] = h
        weighted = h * tpos[1:2, cols]
        total = weighted[:, 0:128]
        for c in range(128, TILE, 128):
            total = total + weighted[:, c:c + 128]
        return total

    def tile(c):
        return pl.ds(pl.multiple_of(c * TILE, TILE), TILE)

    none = jnp.zeros((data_rows, 128), jnp.float32)

    def outputs(stage, total):
        total = jnp.concatenate([total, jnp.zeros((padded - data_rows, 128), jnp.float32)], axis=0)
        flat = jnp.sum(jnp.transpose(total), axis=0, keepdims=True) * out_scale
        part_buf[stage] = jnp.broadcast_to(flat, (8, padded))

        def copy(t, slot):
            return pltpu.make_async_remote_copy(
                part_buf.at[stage], part_all.at[stage, slot], h_ss.at[stage, t], h_rs.at[stage, slot],
                device_id=(me, t), device_id_type=MESH)

        for k in range(1, hids):
            copy(wrap(my_hid + k, hids), my_hid).start()
        part_all[stage, my_hid] = part_buf[stage]
        for k in range(1, hids):
            s = wrap(my_hid + k, hids)
            copy(s, s).wait_recv()
        for k in range(1, hids):
            copy(wrap(my_hid + k, hids), my_hid).wait_send()
        result = part_all[stage, 0]
        for j in range(1, hids):
            result = result + part_all[stage, j]
        return result[0:1]

    def set_resid(result):
        r = TEMPER_LEVEL * NOISE_INV_VARIANCE * (result - tgt_ref[...])
        column = jnp.transpose(jnp.broadcast_to(r, (128, padded)))[0:data_rows]
        for c in range(0, TILE, 128):
            resid[:, c:c + 128] = column

    keep = acc_ref[0] == 1

    def move(first, c, total):
        cols = tile(c)
        h = hid[:, cols]
        b, v = tpos[0:1, cols], tpos[1:2, cols]
        res = resid[...]
        grad_v = jnp.sum(res * h, axis=0, keepdims=True) * out_scale + v
        back = res * (v * out_scale) * (1.0 - h * h)
        grad_b = jnp.sum(back, axis=0, keepdims=True) + b
        grad = lax.dot_general(data_ref[...], back.astype(jnp.bfloat16), (((0,), (0,)), ((), ())),
                               preferred_element_type=jnp.float32) * in_scale
        step = 0.5 * STEP_SIZE if first else STEP_SIZE
        grad_t = jnp.concatenate([grad_b, grad_v], axis=0)
        tm = tmom[0:2, cols] - step * grad_t
        tmom[0:2, cols] = tm
        tpos[0:2, cols] = tpos[0:2, cols] + STEP_SIZE * tinv[0:2, cols] * tm
        inv = mass[:, cols].astype(jnp.float32)
        w0 = theta0[:, cols].astype(jnp.float32)
        if first:
            m = noise_v[:, cols].astype(jnp.float32) * lax.rsqrt(inv) - step * (grad + w0)
            w = w0 + STEP_SIZE * inv * m
            mom[:, cols] = m
            pos[:, cols] = w
        else:
            w = pos[:, cols]
            m = mom[:, cols] - step * (grad + w)
            w = w + STEP_SIZE * inv * m
            moved[:, cols] = jnp.where(keep, w, w0).astype(jnp.bfloat16)
        return total + forward(w.astype(jnp.bfloat16), cols, first)

    start = lax.fori_loop(
        0, width // TILE, lambda c, total: total + forward(theta0[:, tile(c)], tile(c), True), none)
    outputs0 = outputs(0, start)
    set_resid(outputs0)

    noise_copy.wait()
    other = 1 - 2 * inner
    for q in range(half):
        mass_copy(me, 2 * q + 1 - inner, side_ss).wait_recv()

    outputs1 = outputs(1, lax.fori_loop(0, width // TILE, functools.partial(move, True), none))
    set_resid(outputs1)
    last = lax.fori_loop(0, width // TILE, functools.partial(move, False), none)
    result_copy = pltpu.make_async_copy(moved, main_out, loc.at[3])
    result_copy.start()
    outputs2 = outputs(2, last)
    tout[...] = jnp.zeros_like(tout)
    tout[0:2] = jnp.where(keep, tpos[0:2], tpos0[0:2])
    tail_out[...] = tout[...].astype(jnp.bfloat16)
    miss = tgt_ref[...] - jnp.where(keep, outputs2, outputs0)
    fit = jnp.sum(miss * miss, axis=1, keepdims=True) / data_rows
    fit_out[...] = jnp.broadcast_to(fit, fit_out.shape)

    result_copy.wait()
    for k in offsets:
        t = wrap(me + k, groups)
        anc_copy(t, me).wait_send()
        part_copy(t, me).wait_send()
        tail_copy(t, me).wait_send()
        pick_copy(t, me).wait_send()
    for q in range(half):
        who = 2 * q + inner
        mass_copy(me, who, side_ss).wait_send()

        @pl.when((q <= place) & (place < half - 1))
        def _():
            mass_copy(me, who, up_ss).wait_send()

        @pl.when((q >= place) & (place > 0))
        def _():
            mass_copy(me, who, down_ss).wait_send()


def body(groups, hids, particles, noise, ancestors, accepted, data, targets):
    _, rows_all, width = particles.shape
    depth = rows_all - 2
    rows = depth // groups
    data_rows = data.shape[0]
    padded = -(-data_rows // 128) * 128
    anc = jnp.broadcast_to(ancestors[:, None], (1, 128))
    tail = jnp.concatenate(
        [particles[0, depth:], noise[0, depth:], jnp.zeros((12, width), jnp.bfloat16)], axis=0)
    tgt = jnp.pad(targets, (0, padded - data_rows))[None]
    bf, f32 = jnp.bfloat16, jnp.float32
    vm = pl.BlockSpec(memory_space=pltpu.VMEM)
    anywhere = pl.BlockSpec(memory_space=pl.ANY)
    dma = pltpu.SemaphoreType.DMA
    main, last, fit = pl.pallas_call(
        functools.partial(kernel, groups, hids),
        out_shape=(
            jax.ShapeDtypeStruct((depth, width), bf),
            jax.ShapeDtypeStruct((16, width), bf),
            jax.ShapeDtypeStruct((1, 128), f32),
        ),
        in_specs=[vm, pl.BlockSpec(memory_space=pltpu.SMEM), vm, anywhere, anywhere, vm, vm],
        out_specs=(anywhere, vm, vm),
        scratch_shapes=[
            pltpu.VMEM((groups, 1, 128), jnp.int32),
            pltpu.SMEM((groups, 1, 128), jnp.int32),
            pltpu.VMEM((groups, 16, width), bf),
            pltpu.VMEM((groups, rows, width), bf),
            pltpu.VMEM((groups, rows, width), bf),
            pltpu.VMEM((depth, width), bf),
            pltpu.VMEM((depth, width), bf),
            pltpu.VMEM((depth, width), bf),
            pltpu.VMEM((depth, width), f32),
            pltpu.VMEM((depth, width), f32),
            pltpu.VMEM((depth, width), bf),
            pltpu.VMEM((data_rows, width), f32),
            pltpu.VMEM((data_rows, TILE), f32),
            pltpu.VMEM((16, width), f32),
            pltpu.VMEM((16, width), f32),
            pltpu.VMEM((16, width), f32),
            pltpu.VMEM((16, width), f32),
            pltpu.VMEM((16, width), f32),
            pltpu.VMEM((3, 8, padded), f32),
            pltpu.VMEM((3, hids, 8, padded), f32),
        ] + [dma((groups,))] * 8 + [dma((groups,))] * 4 + [dma((3, hids))] * 2 + [dma((4,))],
        compiler_params=pltpu.CompilerParams(
            collective_id=0, has_side_effects=True, vmem_limit_bytes=56 * 1024 * 1024),
        cost_estimate=pl.CostEstimate(
            flops=10 * data_rows * depth * width, bytes_accessed=8 * depth * width,
            transcendentals=3 * data_rows * width),
    )(anc, accepted, tail, particles, noise, data, tgt)
    moved = jnp.concatenate([main, last[:2]], axis=0)[None]
    return moved, fit[0, :1]


def solution(mesh):
    groups, hids = mesh.shape["dom"], mesh.shape["hid"]
    return jax.shard_map(
        functools.partial(body, groups, hids),
        mesh=mesh,
        in_specs=(P("dom", None, "hid"), P("dom", None, "hid"), P("dom"), P("dom"), P(), P()),
        out_specs=(P("dom", None, "hid"), P("dom")),
        check_vma=False,
    )
```

time: 352 us -> 160 us (0.45); the launches traced: 347 us -> 159 us
  Pallas kernels: 0 us -> 149 us
  other arithmetic: 90.7 us -> 3.79 us
  local copies, waits for them, and re-layouts: 80.6 us -> 3.32 us
  blocking collectives: 65.4 us -> 0 us
  waiting for transfers between devices: 59.6 us -> 0 us
  matrix products: 20.9 us -> 0 us
  between operations: 18.3 us -> 3.11 us
  starting transfers between devices: 11.2 us -> 0 us
    pallas_call x0 -> x1, Pallas kernels: none -> 149 us  [body(): pl.pallas_call(functools.partial(kernel, groups, hids), out_shape=(jax.Sh...]
    all_to_all x2 -> x0, waiting for transfers between devices: 59.6 us -> none  [the longest x1 59.6 us: body(): lax.all_to_all(chosen, 'dom', split_axis=0, concat_axis=1, tiled=True)]
    unnamed x1 -> x0, blocking collectives: 46.9 us -> none
    unnamed x32 -> x2, local copies, waits for them, and re-layouts: 34.3 us -> 0.01 us
    sqrt x1 -> x0, other arithmetic: 27.5 us -> none  [body(): momentum = noise.astype(jnp.float32) / jnp.sqrt(inv_mass)[None]]
    concatenate x2 -> x1, local copies, waits for them, and re-layouts: 21.7 us -> 0.08 us  [body(): jnp.concatenate([particles[0, depth:], noise[0, depth:], jnp.zeros((12, w...]
    dot_general x10 -> x0, matrix products: 20.9 us -> none  [the longest x2 11.1 us: potential_gradient(): jnp.einsum('rd,prh->pdh', data, backward.astype(jnp.bfloat16), preferred_...]
    psum x3 -> x0, blocking collectives: 18.6 us -> none  [compute_potential(): network_outputs = lax.psum(partial_value, 'hid')]
  transfers between devices with their start and end apart: 3 -> 0, of which waited for: 1 -> 0; matrix products, arithmetic and copies ran while one was open for 13% -> 0% of each run, Pallas kernels for 0% -> 0%
where the time goes in v1:
time: 160 us; the launch traced here: 159 us
  Pallas kernels  149 us (93%)
  other arithmetic  3.79 us (2%)
  local copies, waits for them, and re-layouts  3.32 us (2%)
  between operations  3.11 us (2%)
    pallas_call x1, Pallas kernels, body(): pl.pallas_call(functools.partial(kernel, groups, hids), out_shape=(jax.Sh...  149 us

profile of v1, /device:TPU:0, one launch (start us, length us, event | category | flops | bytes accessed | tf_op | source)
XLA Modules:
  0.0 159.4 jit_solution(11416244234809244359)
XLA Ops:
  1.9 0.5 broadcast_in_dim.18.anc_ref
  2.4 0.1 pad.9.clone
  2.5 0.7 pad.4
  3.2 0.6 broadcast_in_dim.20.tgt_ref
  3.8 0.7 slice_bitcast_fusion
  4.5 0.7 maximum_maximum_fusion.tail_ref
  5.2 149.2 %shard_map.77 = (bf16[1024,1024]{1,0:T(8,128)(2,1)}, bf16[16,1024]{1,0:T(8,128)(2,1)}, f32[1,128]{1,0:T(1,128)}) custom-call(s32[1,128]{1,0:T(1,128)} %broadcast_in_dim.18.anc_ref, s32[1]{0:T(128)S(6)} %copy.10.acc_ref, bf16[16,1024]{1,0:T(8,128)(2,1)} %maximum_maximum_fusion.tail_ref, bf16[1,1026,1024]{2,1,0:T(8,128)(2,1)} %part_ref.1, ...), custom_call_target="tpu_custom_call" | custom-call | flops 3355443200 | bytes 8388608 | tf_op jit(solution)/shard_map/pallas_call | solution.py:318
  154.4 0.0 copy-start
  154.4 0.7 slice.14
  155.1 3.1 %maximum_bitcast_fusion = bf16[1,1026,1024]{2,1,0:T(8,128)(2,1)} fusion(bf16[2,1024]{1,0:T(2,128)(2,1)S(1)} %slice.14, bf16[1024,1024]{1,0:T(8,128)(2,1)} %get-tuple-element.5), kind=kLoop, calls=%fused_computation | loop fusion | flops 4202496 | bytes 4202496 | tf_op jit(solution)/shard_map/broadcast_in_dim | solution.py:355
  158.2 0.0 copy-done
  (1 shorter events, 0.0 us)
Async XLA Ops:
  154.4 3.8 %copy-start = (f32[1,128]{1,0:T(1,128)S(1)}, f32[1,128]{1,0:T(1,128)}, u32[]{:S(2)}) copy-start(f32[1,128]{1,0:T(1,128)} %get-tuple-element.7) | copy-start | bytes 1540

commit v2 on v1

v2 whole, which is shorter than its diff:
```python
import functools

import jax
import jax.numpy as jnp
from jax import lax
from jax.experimental import pallas as pl
from jax.experimental.pallas import tpu as pltpu
from jax.sharding import PartitionSpec as P

TEMPER_LEVEL = 0.125
NOISE_INV_VARIANCE = 4.0
STEP_SIZE = 0.4
MESH = pl.DeviceIdType.MESH
TILE = 256
CHUNK = 16
CHUNKS = 2


def kernel(
    groups, hids, chunks,
    anc_ref, acc_ref, part_ref, noise_ref, data_ref, tgt_ref,
    main_out, fit_out,
    anc_all, anc_s, tails, recv, picked, theta0, mass, part_v, noise_v, data_t, mom, pos, moved, hid, resid,
    tgt, tpos, tpos0, tmom, tinv, part_buf, part_all,
    anc_ss, anc_rs, tail_ss, tail_rs, p_ss, p_rs, q_ss, q_rs,
    up_ss, down_ss, side_ss, mass_rs, h_ss, h_rs, loc,
):
    me = lax.axis_index("dom")
    my_hid = lax.axis_index("hid")
    depth, width = theta0.shape
    rows = depth // groups
    piece = rows // chunks
    data_rows = data_ref.shape[0]
    padded = part_buf.shape[-1]
    in_scale = depth ** (-0.5)
    out_scale = (width * hids) ** (-0.5)
    half = groups // 2
    offsets = []
    for s in range(groups - 1):
        offsets.append(half + (s + 1) // 2 * (1 if s % 2 else -1))

    def wrap(i, n):
        return lax.rem(i, n)

    def block(i, ch):
        return pl.ds(pl.multiple_of(i * rows + ch * piece, piece), piece)

    part_load = pltpu.make_async_copy(part_ref.at[0], part_v, loc.at[1])
    part_load.start()
    noise_copy = pltpu.make_async_copy(noise_ref.at[0], noise_v, loc.at[0])
    noise_copy.start()
    anc_all[me] = jnp.full((1, 128), anc_ref[0], jnp.int32)

    barrier = pltpu.get_barrier_semaphore()
    for k in range(1, groups):
        pl.semaphore_signal(barrier, inc=1, device_id=(wrap(me + k, groups), my_hid), device_id_type=MESH)
    for k in range(1, hids):
        pl.semaphore_signal(barrier, inc=1, device_id=(me, wrap(my_hid + k, hids)), device_id_type=MESH)
    pl.semaphore_wait(barrier, groups - 1 + hids - 1)

    def anc_copy(t, slot):
        return pltpu.make_async_remote_copy(
            anc_all.at[slot], anc_all.at[slot], anc_ss.at[t], anc_rs.at[slot],
            device_id=(t, my_hid), device_id_type=MESH)

    def tail_copy(t, slot):
        return pltpu.make_async_remote_copy(
            tails.at[slot], tails.at[slot], tail_ss.at[t], tail_rs.at[slot],
            device_id=(t, my_hid), device_id_type=MESH)

    def local_rows(ch):
        return pl.ds(ch * piece, piece)

    def part_copy(t, slot, ch):
        return pltpu.make_async_remote_copy(
            part_ref.at[0, block(t, ch)], recv[ch].at[slot], p_ss.at[ch, t], p_rs.at[ch, slot],
            device_id=(t, my_hid), device_id_type=MESH)

    def pick_copy(t, slot, ch):
        return pltpu.make_async_remote_copy(
            picked.at[t, local_rows(ch)], theta0.at[block(slot, ch)], q_ss.at[ch, t], q_rs.at[ch, slot],
            device_id=(t, my_hid), device_id_type=MESH)

    for k in offsets:
        anc_copy(wrap(me + k, groups), me).start()
    for ch in range(chunks):
        for k in offsets:
            part_copy(wrap(me + k, groups), me, ch).start()

    data_t[...] = jnp.transpose(data_ref[...].astype(jnp.float32)).astype(jnp.bfloat16)
    tgt[...] = jnp.zeros_like(tgt)
    tgt[:, 0:data_rows] = tgt_ref[...]
    part_load.wait()
    tails[me] = jnp.zeros((16, width), jnp.bfloat16)
    tails[me, 0:2] = part_v[depth:depth + 2]
    for k in offsets:
        tail_copy(wrap(me + k, groups), me).start()
    for ch in range(chunks):
        recv[ch][me] = part_v[block(me, ch)]
    noise_copy.wait()

    for k in offsets:
        s = wrap(me + groups - k, groups)
        anc_copy(s, s).wait_recv()
    scalars = pltpu.make_async_copy(anc_all, anc_s, loc.at[2])
    scalars.start()
    scalars.wait()

    shrink = groups / (groups + 5.0)
    floor_term = 0.001 * 5.0 / (groups + 5.0)

    def finish(total, square):
        mean = total / groups
        return (shrink * (square / groups - mean * mean) + floor_term).astype(jnp.bfloat16)

    for k in offsets:
        s = wrap(me + groups - k, groups)
        tail_copy(s, s).wait_recv()

    def add_tail(i, carry):
        total, square = carry
        wide = tails[anc_s[i, 0, 0]].astype(jnp.float32)
        return total + wide, square + wide * wide

    zero = jnp.zeros((16, width), jnp.float32)
    tinv[...] = finish(*lax.fori_loop(0, groups, add_tail, (zero, zero))).astype(jnp.float32)
    tpos0[...] = tails[anc_s[me, 0, 0]].astype(jnp.float32)
    tpos[...] = tpos0[...]
    tmom[0:2] = noise_v[depth:depth + 2].astype(jnp.float32) * lax.rsqrt(tinv[0:2])

    place, inner = me // 2, lax.rem(me, 2)

    def mass_copy(t, who, ch, sem):
        return pltpu.make_async_remote_copy(
            mass.at[block(who, ch)], mass.at[block(who, ch)], sem.at[ch, who], mass_rs.at[ch, who],
            device_id=(t, my_hid), device_id_type=MESH)

    def spread(who, ch, up, down):
        if up:
            @pl.when(place < half - 1)
            def _():
                mass_copy(me + 2, who, ch, up_ss).start()
        if down:
            @pl.when(place > 0)
            def _():
                mass_copy(me - 2, who, ch, down_ss).start()
        mass_copy(me + 1 - 2 * inner, who, ch, side_ss).start()

    def select(ch):
        for k in offsets:
            s = wrap(me + groups - k, groups)
            part_copy(s, s, ch).wait_recv()

        @pl.loop(0, piece // CHUNK)
        def _(r):
            here = pl.ds(pl.multiple_of(ch * piece + r * CHUNK, CHUNK), CHUNK)

            def add(i, carry):
                total, square = carry
                got = recv[ch][anc_s[i, 0, 0], pl.ds(pl.multiple_of(r * CHUNK, CHUNK), CHUNK)]
                picked[i, here] = got
                wide = got.astype(jnp.float32)
                return total + wide, square + wide * wide

            zero = jnp.zeros((CHUNK, width), jnp.float32)
            carry = (zero, zero)
            if groups <= 8:
                for i in range(groups):
                    carry = add(i, carry)
            else:
                carry = lax.fori_loop(0, groups, add, carry)
            there = pl.ds(pl.multiple_of(me * rows + ch * piece + r * CHUNK, CHUNK), CHUNK)
            mass[there] = finish(*carry)
            theta0[there] = picked[me, here]

        spread(me, ch, True, True)
        for k in offsets:
            pick_copy(wrap(me + k, groups), me, ch).start()

    def forward_mass(s, ch):
        @pl.when(place >= s)
        def _():
            mass_copy(me, me - 2 * s, ch, up_ss).wait_recv()
            spread(me - 2 * s, ch, True, False)

        @pl.when(place + s < half)
        def _():
            mass_copy(me, me + 2 * s, ch, up_ss).wait_recv()
            spread(me + 2 * s, ch, False, True)

    for stage in range(chunks + half - 1):
        if stage < chunks:
            select(stage)
        for s in range(1, half):
            if 0 <= stage - s < chunks:
                forward_mass(s, stage - s)

    for ch in range(chunks):
        for k in offsets:
            s = wrap(me + groups - k, groups)
            pick_copy(s, s, ch).wait_recv()

    def forward(weights, cols, keep_hidden):
        pre = jnp.dot(data_ref[...], weights, preferred_element_type=jnp.float32)
        h = jnp.tanh(pre * in_scale + tpos[0:1, cols])
        if keep_hidden:
            hid[:, cols] = h
        weighted = h * tpos[1:2, cols]
        total = weighted[:, 0:128]
        for c in range(128, TILE, 128):
            total = total + weighted[:, c:c + 128]
        return total

    def tile(c):
        return pl.ds(pl.multiple_of(c * TILE, TILE), TILE)

    none = jnp.zeros((data_rows, 128), jnp.float32)
    tiles = width // TILE

    def outputs(stage, total):
        total = jnp.concatenate([total, jnp.zeros((padded - data_rows, 128), jnp.float32)], axis=0)
        flat = jnp.sum(jnp.transpose(total), axis=0, keepdims=True) * out_scale
        part_buf[stage] = jnp.broadcast_to(flat, (8, padded))

        def copy(t, slot):
            return pltpu.make_async_remote_copy(
                part_buf.at[stage], part_all.at[stage, slot], h_ss.at[stage, t], h_rs.at[stage, slot],
                device_id=(me, t), device_id_type=MESH)

        for k in range(1, hids):
            copy(wrap(my_hid + k, hids), my_hid).start()
        part_all[stage, my_hid] = part_buf[stage]
        for k in range(1, hids):
            s = wrap(my_hid + k, hids)
            copy(s, s).wait_recv()
        for k in range(1, hids):
            copy(wrap(my_hid + k, hids), my_hid).wait_send()
        result = part_all[stage, 0]
        for j in range(1, hids):
            result = result + part_all[stage, j]
        return result[0:1]

    def set_resid(result):
        r = TEMPER_LEVEL * NOISE_INV_VARIANCE * (result - tgt[...])
        column = jnp.transpose(jnp.broadcast_to(r, (128, padded)))[0:data_rows]
        for c in range(0, TILE, 128):
            resid[:, c:c + 128] = column

    keep = acc_ref[0] == 1

    def backward(cols, step):
        h = hid[:, cols]
        b, v = tpos[0:1, cols], tpos[1:2, cols]
        res = resid[...]
        grad_v = jnp.sum(res * h, axis=0, keepdims=True) * out_scale + v
        back = res * (v * out_scale) * (1.0 - h * h)
        grad_b = jnp.sum(back, axis=0, keepdims=True) + b
        grad = jnp.dot(data_t[...], back.astype(jnp.bfloat16), preferred_element_type=jnp.float32) * in_scale
        tm = tmom[0:2, cols] - step * jnp.concatenate([grad_b, grad_v], axis=0)
        tmom[0:2, cols] = tm
        tpos[0:2, cols] = tpos[0:2, cols] + STEP_SIZE * tinv[0:2, cols] * tm
        return grad

    start = lax.fori_loop(
        0, tiles, lambda c, total: total + forward(theta0[:, tile(c)], tile(c), True), none)
    outputs0 = outputs(0, start)
    set_resid(outputs0)

    @pl.loop(0, tiles)
    def _(c):
        cols = tile(c)
        mom[:, cols] = backward(cols, 0.5 * STEP_SIZE) + theta0[:, cols].astype(jnp.float32)

    for ch in range(chunks):
        for q in range(half):
            mass_copy(me, 2 * q + 1 - inner, ch, side_ss).wait_recv()

    def first_move(c, total):
        cols = tile(c)
        inv = mass[:, cols].astype(jnp.float32)
        m = noise_v[0:depth, cols].astype(jnp.float32) * lax.rsqrt(inv) - 0.5 * STEP_SIZE * mom[:, cols]
        w = theta0[:, cols].astype(jnp.float32) + STEP_SIZE * inv * m
        mom[:, cols] = m
        pos[:, cols] = w
        return total + forward(w.astype(jnp.bfloat16), cols, True)

    def last_move(c, total):
        cols = tile(c)
        w = pos[:, cols]
        m = mom[:, cols] - STEP_SIZE * (backward(cols, STEP_SIZE) + w)
        w = w + STEP_SIZE * mass[:, cols].astype(jnp.float32) * m
        moved[0:depth, cols] = jnp.where(keep, w, theta0[:, cols].astype(jnp.float32)).astype(jnp.bfloat16)
        return total + forward(w.astype(jnp.bfloat16), cols, False)

    set_resid(outputs(1, lax.fori_loop(0, tiles, first_move, none)))
    last = lax.fori_loop(0, tiles, last_move, none)
    moved[depth:depth + 2] = jnp.where(keep, tpos[0:2], tpos0[0:2]).astype(jnp.bfloat16)
    result_copy = pltpu.make_async_copy(moved, main_out.at[0], loc.at[3])
    result_copy.start()
    outputs2 = outputs(2, last)
    miss = tgt[...] - jnp.where(keep, outputs2, outputs0)
    fit_out[...] = jnp.broadcast_to(jnp.sum(miss * miss, axis=1, keepdims=True) / data_rows, fit_out.shape)

    result_copy.wait()
    for k in offsets:
        t = wrap(me + k, groups)
        anc_copy(t, me).wait_send()
        tail_copy(t, me).wait_send()
    for ch in range(chunks):
        for k in offsets:
            t = wrap(me + k, groups)
            part_copy(t, me, ch).wait_send()
            pick_copy(t, me, ch).wait_send()
        for q in range(half):
            who = 2 * q + inner
            mass_copy(me, who, ch, side_ss).wait_send()

            @pl.when((q <= place) & (place < half - 1))
            def _():
                mass_copy(me, who, ch, up_ss).wait_send()

            @pl.when((q >= place) & (place > 0))
            def _():
                mass_copy(me, who, ch, down_ss).wait_send()


def body(groups, hids, particles, noise, ancestors, accepted, data, targets):
    _, rows_all, width = particles.shape
    depth = rows_all - 2
    rows = depth // groups
    chunks = min(CHUNKS, rows // CHUNK)
    data_rows = data.shape[0]
    padded = -(-data_rows // 128) * 128
    bf, f32 = jnp.bfloat16, jnp.float32
    vm = pl.BlockSpec(memory_space=pltpu.VMEM)
    sm = pl.BlockSpec(memory_space=pltpu.SMEM)
    anywhere = pl.BlockSpec(memory_space=pl.ANY)
    dma = pltpu.SemaphoreType.DMA
    moved, fit = pl.pallas_call(
        functools.partial(kernel, groups, hids, chunks),
        out_shape=(
            jax.ShapeDtypeStruct((1, rows_all, width), bf),
            jax.ShapeDtypeStruct((1, 128), f32),
        ),
        in_specs=[sm, sm, anywhere, anywhere, vm, vm],
        out_specs=(anywhere, vm),
        scratch_shapes=[
            pltpu.VMEM((groups, 1, 128), jnp.int32),
            pltpu.SMEM((groups, 1, 128), jnp.int32),
            pltpu.VMEM((groups, 16, width), bf),
            [pltpu.VMEM((groups, rows // chunks, width), bf)] * chunks,
            pltpu.VMEM((groups, rows, width), bf),
            pltpu.VMEM((depth, width), bf),
            pltpu.VMEM((depth, width), bf),
            pltpu.VMEM((rows_all, width), bf),
            pltpu.VMEM((rows_all, width), bf),
            pltpu.VMEM((depth, data_rows), bf),
            pltpu.VMEM((depth, width), f32),
            pltpu.VMEM((depth, width), f32),
            pltpu.VMEM((rows_all, width), bf),
            pltpu.VMEM((data_rows, width), f32),
            pltpu.VMEM((data_rows, TILE), f32),
            pltpu.VMEM((1, padded), f32),
            pltpu.VMEM((16, width), f32),
            pltpu.VMEM((16, width), f32),
            pltpu.VMEM((16, width), f32),
            pltpu.VMEM((16, width), f32),
            pltpu.VMEM((3, 8, padded), f32),
            pltpu.VMEM((3, hids, 8, padded), f32),
        ] + [dma((groups,))] * 4 + [dma((chunks, groups))] * 8 + [dma((3, hids))] * 2 + [dma((4,))],
        compiler_params=pltpu.CompilerParams(
            collective_id=0, has_side_effects=True, vmem_limit_bytes=56 * 1024 * 1024),
        cost_estimate=pl.CostEstimate(
            flops=10 * data_rows * depth * width, bytes_accessed=8 * depth * width,
            transcendentals=3 * data_rows * width),
    )(ancestors, accepted, particles, noise, data, targets[None])
    return moved, fit[0, :1]


def solution(mesh):
    groups, hids = mesh.shape["dom"], mesh.shape["hid"]
    return jax.shard_map(
        functools.partial(body, groups, hids),
        mesh=mesh,
        in_specs=(P("dom", None, "hid"), P("dom", None, "hid"), P("dom"), P("dom"), P(), P()),
        out_specs=(P("dom", None, "hid"), P("dom")),
        check_vma=False,
    )
```

time: 160 us -> 152 us (0.950)
  Pallas kernels: 149 us -> 144 us
  other arithmetic: 3.79 us -> 0 us
    pallas_call x1, Pallas kernels: 149 us -> 144 us  [body(): pl.pallas_call(functools.partial(kernel, groups, hids, chunks), out_shape...]
    broadcast_in_dim x1 -> x0, other arithmetic: 3.11 us -> none  [body(): moved = jnp.concatenate([main, last[:2]], axis=0)[None]]
    unnamed x2 -> x3, local copies, waits for them, and re-layouts: 0.01 us -> 3.1 us
where the time goes in v2:
time: 152 us; the launch traced here: 151 us
  Pallas kernels  144 us (95%)
  local copies, waits for them, and re-layouts  4.34 us (3%)
  between operations  3.1 us (2%)
    pallas_call x1, Pallas kernels, body(): pl.pallas_call(functools.partial(kernel, groups, hids, chunks), out_shape...  144 us
    unnamed x3, local copies, waits for them, and re-layouts  3.1 us

profile of v2, /device:TPU:0, one launch (start us, length us, event | category | flops | bytes accessed | tf_op | source)
XLA Modules:
  0.0 151.3 jit_solution(13951533388504761479)
XLA Ops:
  1.9 1.2 broadcast_in_dim.3.tgt_ref
  3.2 143.9 %shard_map.77 = (bf16[1,1026,1024]{2,1,0:T(8,128)(2,1)}, f32[1,128]{1,0:T(1,128)}) custom-call(s32[1]{0:T(128)S(6)} %copy.10.anc_ref, s32[1]{0:T(128)S(6)} %copy.11.acc_ref, bf16[1,1026,1024]{2,1,0:T(8,128)(2,1)} %part_ref.1, bf16[1,1026,1024]{2,1,0:T(8,128)(2,1)} %noise_ref.1, bf16[320,1024]{1,0:T(8,128)(2,1)} %data_ref.1, f32[1,320]{1,0:T(1,128)} %broadcast_in_dim.3.tgt_ref), custom_call_target="tpu_custom_call" | custom-call | flops 3355443200 | bytes 8388608 | tf_op jit(solution)/shard_map/pallas_call | solution.py:339
  147.1 0.0 copy-start
  147.1 3.1 %copy.12 = bf16[1,1026,1024]{2,1,0:T(8,128)(2,1)} copy(bf16[1,1026,1024]{2,1,0:T(8,128)(2,1)} %get-tuple-element.8) | data formatting | bytes 4202496
  150.2 0.0 copy-done
Async XLA Ops:
  147.1 3.1 %copy-start = (f32[1,128]{1,0:T(1,128)S(1)}, f32[1,128]{1,0:T(1,128)}, u32[]{:S(2)}) copy-start(f32[1,128]{1,0:T(1,128)} %get-tuple-element.5) | copy-start | bytes 1540

commit v3 on v2

--- a/solution.py
+++ b/solution.py
@@ -174,8 +174,6 @@
             theta0[there] = picked[me, here]
 
         spread(me, ch, True, True)
-        for k in offsets:
-            pick_copy(wrap(me + k, groups), me, ch).start()
 
     def forward_mass(s, ch):
         @pl.when(place >= s)
@@ -188,9 +186,16 @@
             mass_copy(me, me + 2 * s, ch, up_ss).wait_recv()
             spread(me + 2 * s, ch, False, True)
 
-    for stage in range(chunks + half - 1):
+    stages = chunks + half - 1
+    pending = []
+    quota = -(-chunks * (groups - 1) // stages)
+    for stage in range(stages):
         if stage < chunks:
             select(stage)
+            pending += [(k, stage) for k in offsets]
+        for k, ch in pending[:quota]:
+            pick_copy(wrap(me + k, groups), me, ch).start()
+        pending = pending[quota:]
         for s in range(1, half):
             if 0 <= stage - s < chunks:
                 forward_mass(s, stage - s)

time: 152 us -> 150 us (0.987)
  the two profiles are of different devices: /device:TPU:0 before, /device:TPU:3 now
where the time goes in v3:
time: 150 us
  Pallas kernels  143 us (95%)
  local copies, waits for them, and re-layouts  4.34 us (3%)
  between operations  3.1 us (2%)
    pallas_call x1, Pallas kernels, body(): pl.pallas_call(functools.partial(kernel, groups, hids, chunks), out_shape...  143 us
    unnamed x3, local copies, waits for them, and re-layouts  3.1 us

profile of v3, /device:TPU:3, one launch (start us, length us, event | category | flops | bytes accessed | tf_op | source)
XLA Modules:
  0.0 150.1 jit_solution(1929203650972887866)
XLA Ops:
  1.9 1.2 broadcast_in_dim.3.tgt_ref
  3.2 142.6 %shard_map.77 = (bf16[1,1026,1024]{2,1,0:T(8,128)(2,1)}, f32[1,128]{1,0:T(1,128)}) custom-call(s32[1]{0:T(128)S(6)} %copy.10.anc_ref, s32[1]{0:T(128)S(6)} %copy.11.acc_ref, bf16[1,1026,1024]{2,1,0:T(8,128)(2,1)} %part_ref.1, bf16[1,1026,1024]{2,1,0:T(8,128)(2,1)} %noise_ref.1, bf16[320,1024]{1,0:T(8,128)(2,1)} %data_ref.1, f32[1,320]{1,0:T(1,128)} %broadcast_in_dim.3.tgt_ref), custom_call_target="tpu_custom_call" | custom-call | flops 3355443200 | bytes 8388608 | tf_op jit(solution)/shard_map/pallas_call | solution.py:344
  145.8 0.0 copy-start
  145.8 3.1 %copy.12 = bf16[1,1026,1024]{2,1,0:T(8,128)(2,1)} copy(bf16[1,1026,1024]{2,1,0:T(8,128)(2,1)} %get-tuple-element.8) | data formatting | bytes 4202496
  148.9 0.0 copy-done
Async XLA Ops:
  145.8 3.1 %copy-start = (f32[1,128]{1,0:T(1,128)S(1)}, f32[1,128]{1,0:T(1,128)}, u32[]{:S(2)}) copy-start(f32[1,128]{1,0:T(1,128)} %get-tuple-element.5) | copy-start | bytes 1540

commit v4 on v3

--- a/solution.py
+++ b/solution.py
@@ -35,9 +35,22 @@
     in_scale = depth ** (-0.5)
     out_scale = (width * hids) ** (-0.5)
     half = groups // 2
-    offsets = []
-    for s in range(groups - 1):
-        offsets.append(half + (s + 1) // 2 * (1 if s % 2 else -1))
+    offsets = range(1, groups)
+    far, near = list(range(half, groups)), list(range(1, half))
+    far_first = [m for pair in zip(far, near) for m in pair] + far[half - 1:]
+    near_first = [m for pair in zip(near, far) for m in pair] + far[half - 1:]
+
+    def flip(m):
+        t = me
+        for bit in range(groups.bit_length() - 1):
+            if m >> bit & 1:
+                t = t + (1 << bit) - 2 * (1 << bit) * lax.rem(me // (1 << bit), 2)
+        return t
+
+    def target(s):
+        odd = lax.rem(me // 2, 2)
+        first, second = flip(far_first[s]), flip(near_first[s])
+        return first + odd * (second - first)
 
     def wrap(i, n):
         return lax.rem(i, n)
@@ -84,8 +97,8 @@
     for k in offsets:
         anc_copy(wrap(me + k, groups), me).start()
     for ch in range(chunks):
-        for k in offsets:
-            part_copy(wrap(me + k, groups), me, ch).start()
+        for s in range(groups - 1):
+            part_copy(target(s), me, ch).start()
 
     data_t[...] = jnp.transpose(data_ref[...].astype(jnp.float32)).astype(jnp.bfloat16)
     tgt[...] = jnp.zeros_like(tgt)
@@ -192,9 +205,9 @@
     for stage in range(stages):
         if stage < chunks:
             select(stage)
-            pending += [(k, stage) for k in offsets]
-        for k, ch in pending[:quota]:
-            pick_copy(wrap(me + k, groups), me, ch).start()
+            pending += [(s, stage) for s in range(groups - 1)]
+        for s, ch in pending[:quota]:
+            pick_copy(target(s), me, ch).start()
         pending = pending[quota:]
         for s in range(1, half):
             if 0 <= stage - s < chunks:

time: 150 us -> 146 us (0.973)
  the two profiles are of different devices: /device:TPU:3 before, /device:TPU:0 now
where the time goes in v4:
time: 146 us; the launch traced here: 144 us
  Pallas kernels  136 us (93%)
  local copies, waits for them, and re-layouts  4.34 us (3%)
  between operations  3.1 us (2%)
    pallas_call x1, Pallas kernels, body(): pl.pallas_call(functools.partial(kernel, groups, hids, chunks), out_shape...  136 us
    unnamed x3, local copies, waits for them, and re-layouts  3.1 us

profile of v4, /device:TPU:0, one launch (start us, length us, event | category | flops | bytes accessed | tf_op | source)
XLA Modules:
  0.0 143.9 jit_solution(3543265985920718833)
XLA Ops:
  1.9 1.2 broadcast_in_dim.3.tgt_ref
  3.2 136.5 %shard_map.77 = (bf16[1,1026,1024]{2,1,0:T(8,128)(2,1)}, f32[1,128]{1,0:T(1,128)}) custom-call(s32[1]{0:T(128)S(6)} %copy.10.anc_ref, s32[1]{0:T(128)S(6)} %copy.11.acc_ref, bf16[1,1026,1024]{2,1,0:T(8,128)(2,1)} %part_ref.1, bf16[1,1026,1024]{2,1,0:T(8,128)(2,1)} %noise_ref.1, bf16[320,1024]{1,0:T(8,128)(2,1)} %data_ref.1, f32[1,320]{1,0:T(1,128)} %broadcast_in_dim.3.tgt_ref), custom_call_target="tpu_custom_call" | custom-call | flops 3355443200 | bytes 8388608 | tf_op jit(solution)/shard_map/pallas_call | solution.py:357
  139.7 0.0 copy-start
  139.7 3.1 %copy.12 = bf16[1,1026,1024]{2,1,0:T(8,128)(2,1)} copy(bf16[1,1026,1024]{2,1,0:T(8,128)(2,1)} %get-tuple-element.8) | data formatting | bytes 4202496
  142.8 0.0 copy-done
Async XLA Ops:
  139.7 3.1 %copy-start = (f32[1,128]{1,0:T(1,128)S(1)}, f32[1,128]{1,0:T(1,128)}, u32[]{:S(2)}) copy-start(f32[1,128]{1,0:T(1,128)} %get-tuple-element.5) | copy-start | bytes 1540

commit v5 on v4

--- a/solution.py
+++ b/solution.py
@@ -48,7 +48,7 @@
         return t
 
     def target(s):
-        odd = lax.rem(me // 2, 2)
+        odd = lax.rem(me // 2 + my_hid, 2)
         first, second = flip(far_first[s]), flip(near_first[s])
         return first + odd * (second - first)
 
@@ -149,6 +149,10 @@
             device_id=(t, my_hid), device_id_type=MESH)
 
     def spread(who, ch, up, down):
+        @pl.when(lax.rem(my_hid, 2) == 1)
+        def _():
+            mass_copy(me + 1 - 2 * inner, who, ch, side_ss).start()
+
         if up:
             @pl.when(place < half - 1)
             def _():
@@ -157,7 +161,10 @@
             @pl.when(place > 0)
             def _():
                 mass_copy(me - 2, who, ch, down_ss).start()
-        mass_copy(me + 1 - 2 * inner, who, ch, side_ss).start()
+
+        @pl.when(lax.rem(my_hid, 2) == 0)
+        def _():
+            mass_copy(me + 1 - 2 * inner, who, ch, side_ss).start()
 
     def select(ch):
         for k in offsets:
@@ -340,6 +347,17 @@
             @pl.when((q >= place) & (place > 0))
             def _():
                 mass_copy(me, who, ch, down_ss).wait_send()
+
+
+def copy_kernel(parts, in_ref, out_ref, sems):
+    def copy(c):
+        cols = pl.ds(c * TILE, TILE)
+        return pltpu.make_async_copy(in_ref.at[0, :, cols], out_ref.at[0, :, cols], sems.at[c])
+
+    for c in range(parts):
+        copy(c).start()
+    for c in range(parts):
+        copy(c).wait()
 
 
 def body(groups, hids, particles, noise, ancestors, accepted, data, targets):
@@ -392,6 +410,16 @@
             flops=10 * data_rows * depth * width, bytes_accessed=8 * depth * width,
             transcendentals=3 * data_rows * width),
     )(ancestors, accepted, particles, noise, data, targets[None])
+    parts = width // TILE
+    moved = pl.pallas_call(
+        functools.partial(copy_kernel, parts),
+        out_shape=jax.ShapeDtypeStruct(moved.shape, bf),
+        in_specs=[anywhere],
+        out_specs=anywhere,
+        scratch_shapes=[dma((parts,))],
+        cost_estimate=pl.CostEstimate(
+            flops=0, bytes_accessed=4 * rows_all * width, transcendentals=0),
+    )(moved)
     return moved, fit[0, :1]
 
 

time: 146 us -> 208 us (1.42)
  Pallas kernels: 136 us -> 203 us
  local copies, waits for them, and re-layouts: 4.34 us -> 1.25 us
    pallas_call x0 -> x1, Pallas kernels: none -> 65.2 us  [body(): pl.pallas_call(functools.partial(copy_kernel, parts), out_shape=jax.Shape...]
    unnamed x3 -> x2, local copies, waits for them, and re-layouts: 3.1 us -> 0.01 us
where the time goes in v5:
time: 208 us; the launch traced here: 207 us
  Pallas kernels  203 us (98%)
  between operations  3.11 us (1%)
    pallas_call x1, Pallas kernels, body(): pl.pallas_call(functools.partial(kernel, groups, hids, chunks), out_shape...  138 us
    pallas_call x1, Pallas kernels, body(): pl.pallas_call(functools.partial(copy_kernel, parts), out_shape=jax.Shape...  65.2 us

profile of v5, /device:TPU:0, one launch (start us, length us, event | category | flops | bytes accessed | tf_op | source)
XLA Modules:
  0.0 207.5 jit_solution(11631522222997459932)
XLA Ops:
  1.9 1.2 broadcast_in_dim.3.tgt_ref
  3.2 138.0 %shard_map.77 = (bf16[1,1026,1024]{2,1,0:T(8,128)(2,1)}, f32[1,128]{1,0:T(1,128)}) custom-call(s32[1]{0:T(128)S(6)} %copy.9.anc_ref, s32[1]{0:T(128)S(6)} %copy.10.acc_ref, bf16[1,1026,1024]{2,1,0:T(8,128)(2,1)} %part_ref.1, bf16[1,1026,1024]{2,1,0:T(8,128)(2,1)} %noise_ref.1, bf16[320,1024]{1,0:T(8,128)(2,1)} %data_ref.1, f32[1,320]{1,0:T(1,128)} %broadcast_in_dim.3.tgt_ref), custom_call_target="tpu_custom_call" | custom-call | flops 3355443200 | bytes 8388608 | tf_op jit(solution)/shard_map/pallas_call | solution.py:375
  141.1 0.0 copy-start
  141.1 65.2 %shard_map.78 = bf16[1,1026,1024]{2,1,0:T(8,128)(2,1)} custom-call(bf16[1,1026,1024]{2,1,0:T(8,128)(2,1)} %get-tuple-element.4.in_ref), custom_call_target="tpu_custom_call" | custom-call | bytes 4202496 | tf_op jit(solution)/shard_map/pallas_call | solution.py:414
  206.3 0.0 copy-done
Async XLA Ops:
  141.1 65.2 %copy-start = (f32[1,128]{1,0:T(1,128)S(1)}, f32[1,128]{1,0:T(1,128)}, u32[]{:S(2)}) copy-start(f32[1,128]{1,0:T(1,128)} %get-tuple-element.5) | copy-start | bytes 1540

commit v6 on v4

--- a/solution.py
+++ b/solution.py
@@ -48,7 +48,7 @@
         return t
 
     def target(s):
-        odd = lax.rem(me // 2, 2)
+        odd = lax.rem(me // 2 + my_hid, 2)
         first, second = flip(far_first[s]), flip(near_first[s])
         return first + odd * (second - first)
 
@@ -86,7 +86,7 @@
 
     def part_copy(t, slot, ch):
         return pltpu.make_async_remote_copy(
-            part_ref.at[0, block(t, ch)], recv[ch].at[slot], p_ss.at[ch, t], p_rs.at[ch, slot],
+            part_v.at[block(t, ch)], recv[ch].at[slot], p_ss.at[ch, t], p_rs.at[ch, slot],
             device_id=(t, my_hid), device_id_type=MESH)
 
     def pick_copy(t, slot, ch):
@@ -96,6 +96,7 @@
 
     for k in offsets:
         anc_copy(wrap(me + k, groups), me).start()
+    part_load.wait()
     for ch in range(chunks):
         for s in range(groups - 1):
             part_copy(target(s), me, ch).start()
@@ -103,7 +104,6 @@
     data_t[...] = jnp.transpose(data_ref[...].astype(jnp.float32)).astype(jnp.bfloat16)
     tgt[...] = jnp.zeros_like(tgt)
     tgt[:, 0:data_rows] = tgt_ref[...]
-    part_load.wait()
     tails[me] = jnp.zeros((16, width), jnp.bfloat16)
     tails[me, 0:2] = part_v[depth:depth + 2]
     for k in offsets:
@@ -149,6 +149,10 @@
             device_id=(t, my_hid), device_id_type=MESH)
 
     def spread(who, ch, up, down):
+        @pl.when(lax.rem(my_hid, 2) == 1)
+        def _():
+            mass_copy(me + 1 - 2 * inner, who, ch, side_ss).start()
+
         if up:
             @pl.when(place < half - 1)
             def _():
@@ -157,7 +161,10 @@
             @pl.when(place > 0)
             def _():
                 mass_copy(me - 2, who, ch, down_ss).start()
-        mass_copy(me + 1 - 2 * inner, who, ch, side_ss).start()
+
+        @pl.when(lax.rem(my_hid, 2) == 0)
+        def _():
+            mass_copy(me + 1 - 2 * inner, who, ch, side_ss).start()
 
     def select(ch):
         for k in offsets:

time: 146 us -> 146 us (level)
  Pallas kernels: 136 us -> 138 us
where the time goes in v6:
time: 146 us; the launch traced here: 145 us
  Pallas kernels  138 us (95%)
  local copies, waits for them, and re-layouts  4.34 us (3%)
  between operations  3.1 us (2%)
    pallas_call x1, Pallas kernels, body(): pl.pallas_call(functools.partial(kernel, groups, hids, chunks), out_shape...  138 us
    unnamed x3, local copies, waits for them, and re-layouts  3.1 us

profile of v6, /device:TPU:0, one launch (start us, length us, event | category | flops | bytes accessed | tf_op | source)
XLA Modules:
  0.0 145.3 jit_solution(17039817293543227386)
XLA Ops:
  1.9 1.2 broadcast_in_dim.3.tgt_ref
  3.2 137.9 %shard_map.77 = (bf16[1,1026,1024]{2,1,0:T(8,128)(2,1)}, f32[1,128]{1,0:T(1,128)}) custom-call(s32[1]{0:T(128)S(6)} %copy.10.anc_ref, s32[1]{0:T(128)S(6)} %copy.11.acc_ref, bf16[1,1026,1024]{2,1,0:T(8,128)(2,1)} %part_ref.1, bf16[1,1026,1024]{2,1,0:T(8,128)(2,1)} %noise_ref.1, bf16[320,1024]{1,0:T(8,128)(2,1)} %data_ref.1, f32[1,320]{1,0:T(1,128)} %broadcast_in_dim.3.tgt_ref), custom_call_target="tpu_custom_call" | custom-call | flops 3355443200 | bytes 8388608 | tf_op jit(solution)/shard_map/pallas_call | solution.py:364
  141.0 0.0 copy-start
  141.0 3.1 %copy.12 = bf16[1,1026,1024]{2,1,0:T(8,128)(2,1)} copy(bf16[1,1026,1024]{2,1,0:T(8,128)(2,1)} %get-tuple-element.8) | data formatting | bytes 4202496
  144.1 0.0 copy-done
Async XLA Ops:
  141.0 3.1 %copy-start = (f32[1,128]{1,0:T(1,128)S(1)}, f32[1,128]{1,0:T(1,128)}, u32[]{:S(2)}) copy-start(f32[1,128]{1,0:T(1,128)} %get-tuple-element.5) | copy-start | bytes 1540

commit v7 on v6

--- a/solution.py
+++ b/solution.py
@@ -13,7 +13,7 @@
 MESH = pl.DeviceIdType.MESH
 TILE = 256
 CHUNK = 16
-CHUNKS = 2
+CHUNKS = 4
 
 
 def kernel(
@@ -394,7 +394,7 @@
             pltpu.VMEM((3, hids, 8, padded), f32),
         ] + [dma((groups,))] * 4 + [dma((chunks, groups))] * 8 + [dma((3, hids))] * 2 + [dma((4,))],
         compiler_params=pltpu.CompilerParams(
-            collective_id=0, has_side_effects=True, vmem_limit_bytes=56 * 1024 * 1024),
+            collective_id=0, has_side_effects=True, vmem_limit_bytes=34 * 1024 * 1024),
         cost_estimate=pl.CostEstimate(
             flops=10 * data_rows * depth * width, bytes_accessed=8 * depth * width,
             transcendentals=3 * data_rows * width),

time: 146 us -> 150 us (1.027)
  Pallas kernels: 138 us -> 140 us
  local copies, waits for them, and re-layouts: 4.34 us -> 6.29 us
    unnamed x3 -> x7, local copies, waits for them, and re-layouts: 3.1 us -> 5.6 us
    pallas_call x1, Pallas kernels: 138 us -> 140 us  [body(): pl.pallas_call(functools.partial(kernel, groups, hids, chunks), out_shape...]
where the time goes in v7:
time: 150 us
  Pallas kernels  140 us (93%)
  local copies, waits for them, and re-layouts  6.29 us (4%)
  between operations  3.1 us (2%)
    pallas_call x1, Pallas kernels, body(): pl.pallas_call(functools.partial(kernel, groups, hids, chunks), out_shape...  140 us
    unnamed x7, local copies, waits for them, and re-layouts  5.6 us

profile of v7, /device:TPU:0, one launch (start us, length us, event | category | flops | bytes accessed | tf_op | source)
XLA Modules:
  0.0 149.7 jit_solution(11240483742146160848)
XLA Ops:
  1.9 0.7 broadcast_in_dim.3.tgt_ref
  2.6 0.0 copy-start
  2.6 1.6 %copy-done = bf16[1,1026,1024]{2,1,0:T(8,128)(2,1)S(1)} copy-done((bf16[1,1026,1024]{2,1,0:T(8,128)(2,1)S(1)}, bf16[1,1026,1024]{2,1,0:T(8,128)(2,1)}, u32[]{:S(2)}) %copy-start) | copy-done | bytes 2101272
  4.2 0.0 copy-start.1
  4.2 1.6 %copy-done.1 = bf16[1,1026,1024]{2,1,0:T(8,128)(2,1)S(1)} copy-done((bf16[1,1026,1024]{2,1,0:T(8,128)(2,1)S(1)}, bf16[1,1026,1024]{2,1,0:T(8,128)(2,1)}, u32[]{:S(2)}) %copy-start.1) | copy-done | bytes 2101272
  5.8 0.0 copy-start.2
  5.8 1.1 copy-done.2
  6.9 140.3 %shard_map.77 = (bf16[1,1026,1024]{2,1,0:T(8,128)(2,1)S(1)}, f32[1,128]{1,0:T(1,128)S(1)}) custom-call(s32[1]{0:T(128)S(6)} %copy.10.anc_ref, s32[1]{0:T(128)S(6)} %copy.11.acc_ref, bf16[1,1026,1024]{2,1,0:T(8,128)(2,1)S(1)} %copy-done, bf16[1,1026,1024]{2,1,0:T(8,128)(2,1)S(1)} %copy-done.1, bf16[320,1024]{1,0:T(8,128)(2,1)S(1)} %copy-done.2, ...), custom_call_target="tpu_custom_call" | custom-call | flops 3355443200 | bytes 8388608 | tf_op jit(solution)/shard_map/pallas_call | solution.py:364
  147.2 1.3 copy.12
Async XLA Ops:
  2.6 1.6 %copy-start = (bf16[1,1026,1024]{2,1,0:T(8,128)(2,1)S(1)}, bf16[1,1026,1024]{2,1,0:T(8,128)(2,1)}, u32[]{:S(2)}) copy-start(bf16[1,1026,1024]{2,1,0:T(8,128)(2,1)} %part_ref.1) | copy-start | bytes 6303748
  4.2 1.6 %copy-start.1 = (bf16[1,1026,1024]{2,1,0:T(8,128)(2,1)S(1)}, bf16[1,1026,1024]{2,1,0:T(8,128)(2,1)}, u32[]{:S(2)}) copy-start(bf16[1,1026,1024]{2,1,0:T(8,128)(2,1)} %noise_ref.1) | copy-start | bytes 6303748
  5.8 1.1 copy-start.2

commit v8 on v6

--- a/solution.py
+++ b/solution.py
@@ -166,6 +166,95 @@
         def _():
             mass_copy(me + 1 - 2 * inner, who, ch, side_ss).start()
 
+    inward = 1 - 2 * (place // 2)
+    is_end = (place == 0) | (place == half - 1)
+    step = 2 * inward
+    partner = me + 1 - 2 * inner
+
+    def send_own(ch):
+        if half != 4:
+            spread(me, ch, True, True)
+            return
+
+        @pl.when(is_end)
+        def _():
+            mass_copy(me + step, me, ch, up_ss).start()
+            mass_copy(me + 2 * step, me, ch, down_ss).start()
+
+        @pl.when(jnp.logical_not(is_end))
+        def _():
+            mass_copy(me + step, me, ch, up_ss).start()
+            mass_copy(me - step, me, ch, down_ss).start()
+
+        mass_copy(partner, me, ch, side_ss).start()
+
+    def relay(s, ch):
+        @pl.when(is_end)
+        def _():
+            if s == 1:
+                mass_copy(me, partner, ch, up_ss).wait_recv()
+                mass_copy(me + step, partner, ch, up_ss).start()
+            for far_off in ((), (1,), (2, 3))[s - 1]:
+                who = me + far_off * step
+                mass_copy(me, who, ch, up_ss).wait_recv()
+                mass_copy(partner, who, ch, side_ss).start()
+
+        @pl.when(jnp.logical_not(is_end))
+        def _():
+            if s < 3:
+                who = me + s * step
+                mass_copy(me, who, ch, up_ss).wait_recv()
+                mass_copy(me - step, who, ch, down_ss).start()
+                mass_copy(partner, who, ch, side_ss).start()
+
+    def rest_of_mass(ch):
+        if half != 4:
+            for q in range(half):
+                mass_copy(me, 2 * q + 1 - inner, ch, side_ss).wait_recv()
+            return
+
+        @pl.when(is_end)
+        def _():
+            for far_off in (1, 2, 3):
+                mass_copy(me, partner + far_off * step, ch, side_ss).wait_recv()
+
+        @pl.when(jnp.logical_not(is_end))
+        def _():
+            mass_copy(me, me - step, ch, side_ss).wait_recv()
+            mass_copy(me, partner - step, ch, side_ss).wait_recv()
+            for far_off in (0, 1, 2):
+                mass_copy(me, partner + far_off * step, ch, side_ss).wait_recv()
+
+    def mass_sent(ch):
+        if half != 4:
+            for q in range(half):
+                who = 2 * q + inner
+                mass_copy(me, who, ch, side_ss).wait_send()
+
+                @pl.when((q <= place) & (place < half - 1))
+                def _():
+                    mass_copy(me, who, ch, up_ss).wait_send()
+
+                @pl.when((q >= place) & (place > 0))
+                def _():
+                    mass_copy(me, who, ch, down_ss).wait_send()
+            return
+        mass_copy(me, me, ch, up_ss).wait_send()
+        mass_copy(me, me, ch, down_ss).wait_send()
+        mass_copy(me, me, ch, side_ss).wait_send()
+
+        @pl.when(is_end)
+        def _():
+            mass_copy(me, partner, ch, up_ss).wait_send()
+            for far_off in (1, 2, 3):
+                mass_copy(me, me + far_off * step, ch, side_ss).wait_send()
+
+        @pl.when(jnp.logical_not(is_end))
+        def _():
+            for far_off in (1, 2):
+                mass_copy(me, me + far_off * step, ch, side_ss).wait_send()
+                mass_copy(me, me + far_off * step, ch, down_ss).wait_send()
+
     def select(ch):
         for k in offsets:
             s = wrap(me + groups - k, groups)
@@ -193,9 +282,13 @@
             mass[there] = finish(*carry)
             theta0[there] = picked[me, here]
 
-        spread(me, ch, True, True)
+        send_own(ch)
 
     def forward_mass(s, ch):
+        if half == 4:
+            relay(s, ch)
+            return
+
         @pl.when(place >= s)
         def _():
             mass_copy(me, me - 2 * s, ch, up_ss).wait_recv()
@@ -297,8 +390,7 @@
         mom[:, cols] = backward(cols, 0.5 * STEP_SIZE) + theta0[:, cols].astype(jnp.float32)
 
     for ch in range(chunks):
-        for q in range(half):
-            mass_copy(me, 2 * q + 1 - inner, ch, side_ss).wait_recv()
+        rest_of_mass(ch)
 
     def first_move(c, total):
         cols = tile(c)
@@ -336,17 +428,7 @@
             t = wrap(me + k, groups)
             part_copy(t, me, ch).wait_send()
             pick_copy(t, me, ch).wait_send()
-        for q in range(half):
-            who = 2 * q + inner
-            mass_copy(me, who, ch, side_ss).wait_send()
-
-            @pl.when((q <= place) & (place < half - 1))
-            def _():
-                mass_copy(me, who, ch, up_ss).wait_send()
-
-            @pl.when((q >= place) & (place > 0))
-            def _():
-                mass_copy(me, who, ch, down_ss).wait_send()
+        mass_sent(ch)
 
 
 def body(groups, hids, particles, noise, ancestors, accepted, data, targets):

time: 146 us -> 145 us (level)
  Pallas kernels: 138 us -> 136 us
    pallas_call x1, Pallas kernels: 138 us -> 136 us  [body(): pl.pallas_call(functools.partial(kernel, groups, hids, chunks), out_shape...]
where the time goes in v8:
time: 145 us; the launch traced here: 143 us
  Pallas kernels  136 us (94%)
  local copies, waits for them, and re-layouts  4.34 us (3%)
  between operations  3.1 us (2%)
    pallas_call x1, Pallas kernels, body(): pl.pallas_call(functools.partial(kernel, groups, hids, chunks), out_shape...  136 us
    unnamed x3, local copies, waits for them, and re-layouts  3.1 us

profile of v8, /device:TPU:0, one launch (start us, length us, event | category | flops | bytes accessed | tf_op | source)
XLA Modules:
  0.0 143.1 jit_solution(13916578734816095242)
XLA Ops:
  1.9 1.2 broadcast_in_dim.3.tgt_ref
  3.2 135.6 %shard_map.77 = (bf16[1,1026,1024]{2,1,0:T(8,128)(2,1)}, f32[1,128]{1,0:T(1,128)}) custom-call(s32[1]{0:T(128)S(6)} %copy.10.anc_ref, s32[1]{0:T(128)S(6)} %copy.11.acc_ref, bf16[1,1026,1024]{2,1,0:T(8,128)(2,1)} %part_ref.1, bf16[1,1026,1024]{2,1,0:T(8,128)(2,1)} %noise_ref.1, bf16[320,1024]{1,0:T(8,128)(2,1)} %data_ref.1, f32[1,320]{1,0:T(1,128)} %broadcast_in_dim.3.tgt_ref), custom_call_target="tpu_custom_call" | custom-call | flops 3355443200 | bytes 8388608 | tf_op jit(solution)/shard_map/pallas_call | solution.py:446
  138.8 0.0 copy-start
  138.8 3.1 %copy.12 = bf16[1,1026,1024]{2,1,0:T(8,128)(2,1)} copy(bf16[1,1026,1024]{2,1,0:T(8,128)(2,1)} %get-tuple-element.8) | data formatting | bytes 4202496
  141.9 0.0 copy-done
Async XLA Ops:
  138.8 3.1 %copy-start = (f32[1,128]{1,0:T(1,128)S(1)}, f32[1,128]{1,0:T(1,128)}, u32[]{:S(2)}) copy-start(f32[1,128]{1,0:T(1,128)} %get-tuple-element.5) | copy-start | bytes 1540

commit v9 on v8

--- a/solution.py
+++ b/solution.py
@@ -104,8 +104,7 @@
     data_t[...] = jnp.transpose(data_ref[...].astype(jnp.float32)).astype(jnp.bfloat16)
     tgt[...] = jnp.zeros_like(tgt)
     tgt[:, 0:data_rows] = tgt_ref[...]
-    tails[me] = jnp.zeros((16, width), jnp.bfloat16)
-    tails[me, 0:2] = part_v[depth:depth + 2]
+    tails[me] = part_v[depth:depth + 2].astype(jnp.float32)
     for k in offsets:
         tail_copy(wrap(me + k, groups), me).start()
     for ch in range(chunks):
@@ -132,13 +131,13 @@
 
     def add_tail(i, carry):
         total, square = carry
-        wide = tails[anc_s[i, 0, 0]].astype(jnp.float32)
+        wide = tails[anc_s[i, 0, 0]]
         return total + wide, square + wide * wide
 
-    zero = jnp.zeros((16, width), jnp.float32)
-    tinv[...] = finish(*lax.fori_loop(0, groups, add_tail, (zero, zero))).astype(jnp.float32)
-    tpos0[...] = tails[anc_s[me, 0, 0]].astype(jnp.float32)
-    tpos[...] = tpos0[...]
+    zero = jnp.zeros((2, width), jnp.float32)
+    tinv[0:2] = finish(*lax.fori_loop(0, groups, add_tail, (zero, zero))).astype(jnp.float32)
+    tpos0[0:2] = tails[anc_s[me, 0, 0]]
+    tpos[0:2] = tpos0[0:2]
     tmom[0:2] = noise_v[depth:depth + 2].astype(jnp.float32) * lax.rsqrt(tinv[0:2])
 
     place, inner = me // 2, lax.rem(me, 2)
@@ -282,8 +281,6 @@
             mass[there] = finish(*carry)
             theta0[there] = picked[me, here]
 
-        send_own(ch)
-
     def forward_mass(s, ch):
         if half == 4:
             relay(s, ch)
@@ -299,19 +296,28 @@
             mass_copy(me, me + 2 * s, ch, up_ss).wait_recv()
             spread(me + 2 * s, ch, False, True)
 
-    stages = chunks + half - 1
+    def send_picks(some):
+        for s, ch in some:
+            pick_copy(target(s), me, ch).start()
+
+    last_chunk = chunks - 1
     pending = []
-    quota = -(-chunks * (groups - 1) // stages)
-    for stage in range(stages):
-        if stage < chunks:
-            select(stage)
-            pending += [(s, stage) for s in range(groups - 1)]
-        for s, ch in pending[:quota]:
-            pick_copy(target(s), me, ch).start()
+    for ch in range(last_chunk):
+        select(ch)
+        send_own(ch)
+        pending += [(s, ch) for s in range(groups - 1)]
+        send_picks(pending[:3])
+        pending = pending[3:]
+    select(last_chunk)
+    pending += [(s, last_chunk) for s in range(groups - 1)]
+    hops = [(s, ch) for s in range(1, half) for ch in range(last_chunk)]
+    quota = -(-len(pending) // (len(hops) + 1))
+    for s, ch in hops:
+        send_picks(pending[:quota])
         pending = pending[quota:]
-        for s in range(1, half):
-            if 0 <= stage - s < chunks:
-                forward_mass(s, stage - s)
+        forward_mass(s, ch)
+    send_picks(pending)
+    send_own(last_chunk)
 
     for ch in range(chunks):
         for k in offsets:
@@ -383,12 +389,15 @@
         0, tiles, lambda c, total: total + forward(theta0[:, tile(c)], tile(c), True), none)
     outputs0 = outputs(0, start)
     set_resid(outputs0)
+    forward_mass(1, last_chunk)
 
     @pl.loop(0, tiles)
     def _(c):
         cols = tile(c)
         mom[:, cols] = backward(cols, 0.5 * STEP_SIZE) + theta0[:, cols].astype(jnp.float32)
 
+    for s in range(2, half):
+        forward_mass(s, last_chunk)
     for ch in range(chunks):
         rest_of_mass(ch)
 
@@ -454,7 +463,7 @@
         scratch_shapes=[
             pltpu.VMEM((groups, 1, 128), jnp.int32),
             pltpu.SMEM((groups, 1, 128), jnp.int32),
-            pltpu.VMEM((groups, 16, width), bf),
+            pltpu.VMEM((groups, 2, width), f32),
             [pltpu.VMEM((groups, rows // chunks, width), bf)] * chunks,
             pltpu.VMEM((groups, rows, width), bf),
             pltpu.VMEM((depth, width), bf),
@@ -468,10 +477,10 @@
             pltpu.VMEM((data_rows, width), f32),
             pltpu.VMEM((data_rows, TILE), f32),
             pltpu.VMEM((1, padded), f32),
-            pltpu.VMEM((16, width), f32),
-            pltpu.VMEM((16, width), f32),
-            pltpu.VMEM((16, width), f32),
-            pltpu.VMEM((16, width), f32),
+            pltpu.VMEM((8, width), f32),
+            pltpu.VMEM((8, width), f32),
+            pltpu.VMEM((8, width), f32),
+            pltpu.VMEM((8, width), f32),
             pltpu.VMEM((3, 8, padded), f32),
             pltpu.VMEM((3, hids, 8, padded), f32),
         ] + [dma((groups,))] * 4 + [dma((chunks, groups))] * 8 + [dma((3, hids))] * 2 + [dma((4,))],

time: 145 us -> 151 us (1.041); the launches traced: 143 us -> 151 us
  Pallas kernels: 136 us -> 143 us
    pallas_call x1, Pallas kernels: 136 us -> 143 us  [body(): pl.pallas_call(functools.partial(kernel, groups, hids, chunks), out_shape...]
where the time goes in v9:
time: 151 us
  Pallas kernels  143 us (95%)
  local copies, waits for them, and re-layouts  4.34 us (3%)
  between operations  3.1 us (2%)
    pallas_call x1, Pallas kernels, body(): pl.pallas_call(functools.partial(kernel, groups, hids, chunks), out_shape...  143 us
    unnamed x3, local copies, waits for them, and re-layouts  3.1 us

profile of v9, /device:TPU:0, one launch (start us, length us, event | category | flops | bytes accessed | tf_op | source)
XLA Modules:
  0.0 150.7 jit_solution(12261652902473170587)
XLA Ops:
  1.9 1.2 broadcast_in_dim.3.tgt_ref
  3.2 143.2 %shard_map.77 = (bf16[1,1026,1024]{2,1,0:T(8,128)(2,1)}, f32[1,128]{1,0:T(1,128)}) custom-call(s32[1]{0:T(128)S(6)} %copy.10.anc_ref, s32[1]{0:T(128)S(6)} %copy.11.acc_ref, bf16[1,1026,1024]{2,1,0:T(8,128)(2,1)} %part_ref.1, bf16[1,1026,1024]{2,1,0:T(8,128)(2,1)} %noise_ref.1, bf16[320,1024]{1,0:T(8,128)(2,1)} %data_ref.1, f32[1,320]{1,0:T(1,128)} %broadcast_in_dim.3.tgt_ref), custom_call_target="tpu_custom_call" | custom-call | flops 3355443200 | bytes 8388608 | tf_op jit(solution)/shard_map/pallas_call | solution.py:455
  146.4 0.0 copy-start
  146.4 3.1 %copy.12 = bf16[1,1026,1024]{2,1,0:T(8,128)(2,1)} copy(bf16[1,1026,1024]{2,1,0:T(8,128)(2,1)} %get-tuple-element.8) | data formatting | bytes 4202496
  149.5 0.0 copy-done
Async XLA Ops:
  146.4 3.1 %copy-start = (f32[1,128]{1,0:T(1,128)S(1)}, f32[1,128]{1,0:T(1,128)}, u32[]{:S(2)}) copy-start(f32[1,128]{1,0:T(1,128)} %get-tuple-element.5) | copy-start | bytes 1540

commit v10 on v8

--- a/solution.py
+++ b/solution.py
@@ -104,8 +104,7 @@
     data_t[...] = jnp.transpose(data_ref[...].astype(jnp.float32)).astype(jnp.bfloat16)
     tgt[...] = jnp.zeros_like(tgt)
     tgt[:, 0:data_rows] = tgt_ref[...]
-    tails[me] = jnp.zeros((16, width), jnp.bfloat16)
-    tails[me, 0:2] = part_v[depth:depth + 2]
+    tails[me] = part_v[depth:depth + 2].astype(jnp.float32)
     for k in offsets:
         tail_copy(wrap(me + k, groups), me).start()
     for ch in range(chunks):
@@ -132,13 +131,13 @@
 
     def add_tail(i, carry):
         total, square = carry
-        wide = tails[anc_s[i, 0, 0]].astype(jnp.float32)
+        wide = tails[anc_s[i, 0, 0]]
         return total + wide, square + wide * wide
 
-    zero = jnp.zeros((16, width), jnp.float32)
-    tinv[...] = finish(*lax.fori_loop(0, groups, add_tail, (zero, zero))).astype(jnp.float32)
-    tpos0[...] = tails[anc_s[me, 0, 0]].astype(jnp.float32)
-    tpos[...] = tpos0[...]
+    zero = jnp.zeros((2, width), jnp.float32)
+    tinv[0:2] = finish(*lax.fori_loop(0, groups, add_tail, (zero, zero))).astype(jnp.float32)
+    tpos0[0:2] = tails[anc_s[me, 0, 0]]
+    tpos[0:2] = tpos0[0:2]
     tmom[0:2] = noise_v[depth:depth + 2].astype(jnp.float32) * lax.rsqrt(tinv[0:2])
 
     place, inner = me // 2, lax.rem(me, 2)
@@ -454,7 +453,7 @@
         scratch_shapes=[
             pltpu.VMEM((groups, 1, 128), jnp.int32),
             pltpu.SMEM((groups, 1, 128), jnp.int32),
-            pltpu.VMEM((groups, 16, width), bf),
+            pltpu.VMEM((groups, 2, width), f32),
             [pltpu.VMEM((groups, rows // chunks, width), bf)] * chunks,
             pltpu.VMEM((groups, rows, width), bf),
             pltpu.VMEM((depth, width), bf),
@@ -468,10 +467,10 @@
             pltpu.VMEM((data_rows, width), f32),
             pltpu.VMEM((data_rows, TILE), f32),
             pltpu.VMEM((1, padded), f32),
-            pltpu.VMEM((16, width), f32),
-            pltpu.VMEM((16, width), f32),
-            pltpu.VMEM((16, width), f32),
-            pltpu.VMEM((16, width), f32),
+            pltpu.VMEM((8, width), f32),
+            pltpu.VMEM((8, width), f32),
+            pltpu.VMEM((8, width), f32),
+            pltpu.VMEM((8, width), f32),
             pltpu.VMEM((3, 8, padded), f32),
             pltpu.VMEM((3, hids, 8, padded), f32),
         ] + [dma((groups,))] * 4 + [dma((chunks, groups))] * 8 + [dma((3, hids))] * 2 + [dma((4,))],

time: 145 us -> 141 us (0.972)
  Pallas kernels: 136 us -> 132 us
    pallas_call x1, Pallas kernels: 136 us -> 132 us  [body(): pl.pallas_call(functools.partial(kernel, groups, hids, chunks), out_shape...]
where the time goes in v10:
time: 141 us; the launch traced here: 139 us
  Pallas kernels  132 us (94%)
  local copies, waits for them, and re-layouts  4.34 us (3%)
  between operations  3.1 us (2%)
    pallas_call x1, Pallas kernels, body(): pl.pallas_call(functools.partial(kernel, groups, hids, chunks), out_shape...  132 us
    unnamed x3, local copies, waits for them, and re-layouts  3.1 us

profile of v10, /device:TPU:0, one launch (start us, length us, event | category | flops | bytes accessed | tf_op | source)
XLA Modules:
  0.0 139.2 jit_solution(13542462179428684934)
XLA Ops:
  1.9 1.2 broadcast_in_dim.3.tgt_ref
  3.2 131.8 %shard_map.77 = (bf16[1,1026,1024]{2,1,0:T(8,128)(2,1)}, f32[1,128]{1,0:T(1,128)}) custom-call(s32[1]{0:T(128)S(6)} %copy.10.anc_ref, s32[1]{0:T(128)S(6)} %copy.11.acc_ref, bf16[1,1026,1024]{2,1,0:T(8,128)(2,1)} %part_ref.1, bf16[1,1026,1024]{2,1,0:T(8,128)(2,1)} %noise_ref.1, bf16[320,1024]{1,0:T(8,128)(2,1)} %data_ref.1, f32[1,320]{1,0:T(1,128)} %broadcast_in_dim.3.tgt_ref), custom_call_target="tpu_custom_call" | custom-call | flops 3355443200 | bytes 8388608 | tf_op jit(solution)/shard_map/pallas_call | solution.py:445
  135.0 0.0 copy-start
  135.0 3.1 %copy.12 = bf16[1,1026,1024]{2,1,0:T(8,128)(2,1)} copy(bf16[1,1026,1024]{2,1,0:T(8,128)(2,1)} %get-tuple-element.8) | data formatting | bytes 4202496
  138.1 0.0 copy-done
Async XLA Ops:
  135.0 3.1 %copy-start = (f32[1,128]{1,0:T(1,128)S(1)}, f32[1,128]{1,0:T(1,128)}, u32[]{:S(2)}) copy-start(f32[1,128]{1,0:T(1,128)} %get-tuple-element.5) | copy-start | bytes 1540
